TPU v7x, 32 devices: a whole 2x2x4 slice. The times are simulated.
32 devices in a mesh: samp: 4 (over y, core), sp: 8 (over z, x).
Axes of the slice: x: 2, y: 2, z: 4, core: 2. Of those that a mesh axis runs over, the one named last changes fastest.
Arguments:
- tokens: bfloat16 [4, 96, 160, 768], P('samp', 'sp'), may hold values from -6 to 6
- cotangent: bfloat16 [4, 96, 160, 768], P('samp', 'sp'), may hold values from -6 to 6
- storm_weight: int32 [4], P('samp'), may hold values from 16 to 192
- filter_master: float32 [768, 384], P(('samp', 'sp')), may hold values from -0.4375 to 0.4375
- in_master: float32 [768, 3072], P(('samp', 'sp')), may hold values from -0.21875 to 0.21875
- out_master: float32 [3072, 768], P(('samp', 'sp')), may hold values from -0.109375 to 0.109375
- small_master: float32 [9984], P(('samp', 'sp')), may hold values from -1.2 to 1.6, as said below
- filter_m: float32 [768, 384], P(('samp', 'sp')), may hold values from -128 to 128
- filter_v: float32 [768, 384], P(('samp', 'sp')), may hold values from 1536 to 6144
- in_m: float32 [768, 3072], P(('samp', 'sp')), may hold values from -96 to 96
- in_v: float32 [768, 3072], P(('samp', 'sp')), may hold values from 921.6 to 3686.4
- out_m: float32 [3072, 768], P(('samp', 'sp')), may hold values from -192 to 192
- out_v: float32 [3072, 768], P(('samp', 'sp')), may hold values from 4300.8 to 17203.2
- small_m: float32 [9984], P(('samp', 'sp')), may hold values from -160 to 160
- small_v: float32 [9984], P(('samp', 'sp')), may hold values from 3072 to 12288
- filter_ema: float32 [768, 384], P(('samp', 'sp')), may hold values from -0.4375 to 0.4375
- in_ema: float32 [768, 3072], P(('samp', 'sp')), may hold values from -0.21875 to 0.21875
- out_ema: float32 [3072, 768], P(('samp', 'sp')), may hold values from -0.109375 to 0.109375
- small_ema: float32 [9984], P(('samp', 'sp')), may hold values from 0.5 to 1.5
Outputs:
- result: bfloat16 [4, 96, 160, 768], P('samp', 'sp')
- input_grad: float32 [4, 96, 160, 768], P('samp', 'sp')
- filter_grad: float32 [768, 384], P(('samp', 'sp'))
- in_grad: float32 [768, 3072], P(('samp', 'sp'))
- out_grad: float32 [3072, 768], P(('samp', 'sp'))
- small_grad: float32 [9984], P(('samp', 'sp'))
- filter_new: float32 [768, 384], P(('samp', 'sp'))
- in_new: float32 [768, 3072], P(('samp', 'sp'))
- out_new: float32 [3072, 768], P(('samp', 'sp'))
- small_new: float32 [9984], P(('samp', 'sp'))
- filter_m_new: float32 [768, 384], P(('samp', 'sp'))
- filter_v_new: float32 [768, 384], P(('samp', 'sp'))
- in_m_new: float32 [768, 3072], P(('samp', 'sp'))
- in_v_new: float32 [768, 3072], P(('samp', 'sp'))
- out_m_new: float32 [3072, 768], P(('samp', 'sp'))
- out_v_new: float32 [3072, 768], P(('samp', 'sp'))
- small_m_new: float32 [9984], P(('samp', 'sp'))
- small_v_new: float32 [9984], P(('samp', 'sp'))
- filter_ema_new: float32 [768, 384], P(('samp', 'sp'))
- in_ema_new: float32 [768, 3072], P(('samp', 'sp'))
- out_ema_new: float32 [3072, 768], P(('samp', 'sp'))
- small_ema_new: float32 [9984], P(('samp', 'sp'))
Inputs may be any that keep to these rules, and one draw needn't show every extreme that they name: `small_master`: rows 0 and 2 of the small vector are gains, the others biases.
All inputs are finite; a program needn't handle non-finite values.
Results may differ from a plain program's by a relative error of at most 0.014.
Values may be sent and summed in bfloat16 or wider, within the bound.
No kernel may reach another device: no remote copies, remote signals or barrier semaphores. Data moves between devices by JAX's collectives and lax.ppermute only.
A program may use at most 320 MiB of HBM per device.

v0:
```python
import functools
import math

import jax
import jax.numpy as jnp
import numpy as np
from jax import lax
from jax.experimental import pallas as pl
from jax.experimental.pallas import tpu as pltpu
from jax.sharding import Mesh
from jax.sharding import PartitionSpec as P

NB = 8
STEP = 10


HIGHEST = lax.Precision.HIGHEST
NORM_EPS = 1e-05
BETA_ONE = 0.9
BETA_TWO = 0.95
ADAM_EPS = 1e-08
DECAY = 0.05
EMA_KEEP = 0.75


def gelu_exact(values):
    return jax.nn.gelu(values, approximate=False)


def norm_forward(values):
    center = values - jnp.mean(values, axis=-1, keepdims=True)
    inv_std = lax.rsqrt(jnp.mean(center * center, axis=-1, keepdims=True) + NORM_EPS)
    return (center * inv_std, inv_std)


def norm_back(upstream, normed, inv_std, gain):
    scaled = upstream * gain
    first_mean = jnp.mean(scaled, axis=-1, keepdims=True)
    second_mean = jnp.mean(scaled * normed, axis=-1, keepdims=True)
    leading = tuple(range(upstream.ndim - 1))
    input_part = inv_std * (scaled - first_mean - normed * second_mean)
    return (input_part, jnp.sum(upstream * normed, axis=leading), jnp.sum(upstream, axis=leading))


def dft_table(points):
    positions = jnp.arange(points, dtype=jnp.int32)
    phases = positions[:, None] * positions[None, :] % points
    angles = phases.astype(jnp.float32) * (2.0 * math.pi / points)
    factor = 1.0 / math.sqrt(points)
    return (jnp.cos(angles) * factor, jnp.sin(angles) * factor)


def lat_table(cosine, sine_part, sign_value):
    upper_rows = jnp.stack([cosine, -sign_value * sine_part], axis=-1)
    lower_rows = jnp.stack([sign_value * sine_part, cosine], axis=-1)
    return jnp.stack([upper_rows, lower_rows], axis=1)


def split_table(table):
    upper_part = table.astype(jnp.bfloat16)
    lower_part = (table - upper_part.astype(jnp.float32)).astype(jnp.bfloat16)
    return (upper_part, lower_part)


def table_first(form, table, values):
    upper_part, lower_part = split_table(table)
    return jnp.einsum(form, upper_part, values, preferred_element_type=jnp.float32) + jnp.einsum(
        form, lower_part, values, preferred_element_type=jnp.float32
    )


def table_second(form, values, table):
    upper_part, lower_part = split_table(table)
    return jnp.einsum(form, values, upper_part, preferred_element_type=jnp.float32) + jnp.einsum(
        form, values, lower_part, preferred_element_type=jnp.float32
    )


def complex_mix(inputs, weight):
    shape_in = inputs.shape
    size_block = weight.shape[1] // 2
    grouped = inputs.reshape(shape_in[:4] + (NB, size_block))
    matrices = weight.reshape(NB, size_block, 2, size_block)
    product = jnp.einsum(
        "sgckbi,bieo->sgcekbo", grouped, matrices, preferred_element_type=jnp.float32
    )
    real_part = product[:, :, 0, 0] - product[:, :, 1, 1]
    imag_part = product[:, :, 1, 0] + product[:, :, 0, 1]
    return jnp.stack([real_part, imag_part], axis=2).reshape(shape_in)


def mix_back(upstream, inputs, weight):
    shape_in = inputs.shape
    size_block = weight.shape[1] // 2
    grouped = inputs.reshape(shape_in[:4] + (NB, size_block))
    upstream_grouped = upstream.reshape(shape_in[:4] + (NB, size_block))
    matrices = weight.reshape(NB, size_block, 2, size_block)
    toward = jnp.einsum(
        "sgekbo,bico->sgeckbi", upstream_grouped, matrices, preferred_element_type=jnp.float32
    )
    grad_real = toward[:, :, 0, 0] + toward[:, :, 1, 1]
    grad_imag = toward[:, :, 1, 0] - toward[:, :, 0, 1]
    grad_inputs = jnp.stack([grad_real, grad_imag], axis=2).reshape(shape_in)
    outer_sums = jnp.einsum(
        "sgckbi,sgekbo->cebio", grouped, upstream_grouped, preferred_element_type=jnp.float32
    )
    weight_real = outer_sums[0, 0] + outer_sums[1, 1]
    weight_imag = outer_sums[0, 1] - outer_sums[1, 0]
    weight_grad = jnp.stack([weight_real, weight_imag], axis=2).reshape(weight.shape)
    bias_grad = jnp.sum(upstream, axis=(0, 1, 3), dtype=jnp.float32)
    return (grad_inputs, weight_grad, bias_grad)


def adam_update(master, gradient, moment, second, average, step_rate):
    moment_new = BETA_ONE * moment + (1.0 - BETA_ONE) * gradient
    second_new = BETA_TWO * second + (1.0 - BETA_TWO) * gradient * gradient
    scaled_moment = moment_new / (1.0 - BETA_ONE**STEP)
    scaled_second = second_new / (1.0 - BETA_TWO**STEP)
    master_new = master - step_rate * (
        scaled_moment / (jnp.sqrt(scaled_second) + ADAM_EPS) + DECAY * master
    )
    average_new = EMA_KEEP * average + (1.0 - EMA_KEEP) * master_new
    return (master_new, moment_new, second_new, average_new)


def plain_shards(
    tokens,
    cotangent,
    storm_weight,
    filter_master,
    in_master,
    out_master,
    small_master,
    filter_m,
    filter_v,
    in_m,
    in_v,
    out_m,
    out_v,
    small_m,
    small_v,
    filter_ema,
    in_ema,
    out_ema,
    small_ema,
):
    filter_work, small_work = (
        lax.all_gather(filter_master.astype(jnp.bfloat16), ("samp", "sp"), axis=0, tiled=True),
        lax.all_gather(small_master.astype(jnp.bfloat16), ("samp", "sp"), axis=0, tiled=True),
    )
    width = filter_work.shape[0]
    size_block = width // NB
    params = small_work.astype(jnp.float32).reshape(13, width)
    inputs = tokens.astype(jnp.float32)
    normed_one, inv_one = norm_forward(inputs)
    first = normed_one * params[0] + params[1]
    lon_cos, lon_sin = dft_table(tokens.shape[2])
    lon_forward = jnp.stack([lon_cos, -lon_sin], axis=1)
    lon_inverse = jnp.stack([lon_cos, -lon_sin], axis=0)
    spectrum = jnp.einsum("shwd,wck->shckd", first, lon_forward, precision=HIGHEST).astype(
        jnp.bfloat16
    )
    arrived = lax.all_to_all(spectrum, "sp", split_axis=3, concat_axis=1, tiled=True)
    lat_cos, lat_sin = dft_table(arrived.shape[1])
    lat_forward = lat_table(lat_cos, lat_sin, -1.0)
    lat_inverse = lat_table(lat_cos, lat_sin, 1.0)
    modes = table_first("gohc,shckd->sgokd", lat_forward, arrived).astype(jnp.bfloat16)
    bias_one = params[4:6][:, None, :]
    bias_two = params[6:8][:, None, :]
    pre_one = complex_mix(modes, filter_work[:, : 2 * size_block]) + bias_one
    hidden_one = gelu_exact(pre_one).astype(jnp.bfloat16)
    pre_two = complex_mix(hidden_one, filter_work[:, 2 * size_block :]) + bias_two
    leaving = jnp.einsum("gohc,shckd->sgokd", lat_inverse, pre_two, precision=HIGHEST).astype(
        jnp.bfloat16
    )
    returned = lax.all_to_all(leaving, "sp", split_axis=1, concat_axis=3, tiled=True)
    spatial = table_second("shckd,ckw->shwd", returned, lon_inverse)
    mixed = spatial + first + inputs
    in_work, out_work = (
        lax.all_gather(in_master.astype(jnp.bfloat16), ("samp", "sp"), axis=0, tiled=True),
        lax.all_gather(out_master.astype(jnp.bfloat16), ("samp", "sp"), axis=0, tiled=True),
    )
    normed_two, inv_two = norm_forward(mixed)
    second = (normed_two * params[2] + params[3]).astype(jnp.bfloat16).reshape(-1, width)
    pre_dense = jnp.dot(second, in_work, preferred_element_type=jnp.float32) + params[9:13].reshape(
        -1
    )
    act_dense = gelu_exact(pre_dense).astype(jnp.bfloat16)
    branch = jnp.dot(act_dense, out_work, preferred_element_type=jnp.float32) + params[8]
    result = (mixed + branch.reshape(mixed.shape)).astype(jnp.bfloat16)
    filter_back = lax.all_gather(
        filter_master.astype(jnp.bfloat16), ("samp", "sp"), axis=0, tiled=True
    )
    in_back, out_back = (
        lax.all_gather(in_master.astype(jnp.bfloat16), ("samp", "sp"), axis=0, tiled=True),
        lax.all_gather(out_master.astype(jnp.bfloat16), ("samp", "sp"), axis=0, tiled=True),
    )
    sample_scale = storm_weight.astype(jnp.float32)[:, None, None, None] / 64.0
    grad_out = cotangent.astype(jnp.float32) * sample_scale
    grad_low = grad_out.astype(jnp.bfloat16).reshape(-1, width)
    out_local = jnp.einsum("tf,td->fd", act_dense, grad_low, preferred_element_type=jnp.float32)
    out_bias_grad = jnp.sum(grad_low, axis=0, dtype=jnp.float32)
    grad_act = jnp.einsum("td,fd->tf", grad_low, out_back, preferred_element_type=jnp.float32)
    dense_values, dense_pull = jax.vjp(gelu_exact, pre_dense)
    grad_pre = dense_pull(grad_act)[0].astype(jnp.bfloat16)
    in_local = jnp.einsum("td,tf->df", second, grad_pre, preferred_element_type=jnp.float32)
    in_bias_grad = jnp.sum(grad_pre, axis=0, dtype=jnp.float32)
    grad_second = jnp.einsum(
        "tf,df->td", grad_pre, in_back, preferred_element_type=jnp.float32
    ).reshape(mixed.shape)
    grad_norm_two, gain_two_grad, shift_two_grad = norm_back(
        grad_second, normed_two, inv_two, params[2]
    )
    grad_mixed = grad_out + grad_norm_two
    grad_leaving = jnp.einsum("shwd,ckw->shckd", grad_mixed, lon_inverse, precision=HIGHEST).astype(
        jnp.bfloat16
    )
    grad_arrived = lax.all_to_all(grad_leaving, "sp", split_axis=3, concat_axis=1, tiled=True)
    grad_pre_two = table_first("gohc,sgokd->shckd", lat_inverse, grad_arrived).astype(jnp.bfloat16)
    grad_hidden, weight_two_grad, bias_two_grad = mix_back(
        grad_pre_two, hidden_one, filter_back[:, 2 * size_block :]
    )
    gelu_values, gelu_pull = jax.vjp(gelu_exact, pre_one)
    grad_pre_one = gelu_pull(grad_hidden)[0].astype(jnp.bfloat16)
    grad_modes, weight_one_grad, bias_one_grad = mix_back(
        grad_pre_one, modes, filter_back[:, : 2 * size_block]
    )
    grad_spectrum = jnp.einsum(
        "gohc,sgokd->shckd", lat_forward, grad_modes, precision=HIGHEST
    ).astype(jnp.bfloat16)
    grad_sent = lax.all_to_all(grad_spectrum, "sp", split_axis=1, concat_axis=3, tiled=True)
    grad_first = grad_mixed + table_second("shckd,wck->shwd", grad_sent, lon_forward)
    grad_norm_one, gain_one_grad, shift_one_grad = norm_back(
        grad_first, normed_one, inv_one, params[0]
    )
    input_grad = grad_mixed + grad_norm_one
    norm_rows = jnp.stack([gain_one_grad, shift_one_grad, gain_two_grad, shift_two_grad])
    small_local = jnp.concatenate(
        [
            norm_rows,
            bias_one_grad,
            bias_two_grad,
            out_bias_grad[None, :],
            in_bias_grad.reshape(-1, width),
        ],
        axis=0,
    ).reshape(-1)
    filter_local = jnp.concatenate([weight_one_grad, weight_two_grad], axis=1)
    filter_grad, in_grad, out_grad, small_grad = (
        lax.psum_scatter(filter_local, ("samp", "sp"), scatter_dimension=0, tiled=True),
        lax.psum_scatter(in_local, ("samp", "sp"), scatter_dimension=0, tiled=True),
        lax.psum_scatter(out_local, ("samp", "sp"), scatter_dimension=0, tiled=True),
        lax.psum_scatter(small_local, ("samp", "sp"), scatter_dimension=0, tiled=True),
    )
    filter_new, filter_m_new, filter_v_new, filter_ema_new = adam_update(
        filter_master, filter_grad, filter_m, filter_v, filter_ema, 0.2
    )
    in_new, in_m_new, in_v_new, in_ema_new = adam_update(
        in_master, in_grad, in_m, in_v, in_ema, 0.1
    )
    out_new, out_m_new, out_v_new, out_ema_new = adam_update(
        out_master, out_grad, out_m, out_v, out_ema, 0.05
    )
    small_new, small_m_new, small_v_new, small_ema_new = adam_update(
        small_master, small_grad, small_m, small_v, small_ema, 0.5
    )
    return (
        result,
        input_grad,
        filter_grad,
        in_grad,
        out_grad,
        small_grad,
        filter_new,
        in_new,
        out_new,
        small_new,
        filter_m_new,
        filter_v_new,
        in_m_new,
        in_v_new,
        out_m_new,
        out_v_new,
        small_m_new,
        small_v_new,
        filter_ema_new,
        in_ema_new,
        out_ema_new,
        small_ema_new,
    )


F32 = jnp.float32
BF16 = jnp.bfloat16
LAT = 96
LON = 160
GROUP = 4
HALF = 384
ROWS = 208
FCHUNK = 512
VMEM_BYTES = 56 * 1024 * 1024
SCHED = pltpu.CompilerParams(vmem_limit_bytes=VMEM_BYTES)


def fits(sizes):
    parts = sizes[1]
    return sizes == (4, 8) and LAT % (parts * GROUP) == 0 and LON // 2 % (2 * parts) == 0


def cost(time_us, bytes_moved):
    return pl.CostEstimate(
        flops=int(time_us * 1.15e9), bytes_accessed=bytes_moved, transcendentals=0
    )


def dot(left, right, left_dim, right_dim):
    return lax.dot_general(
        left, right, (((left_dim,), (right_dim,)), ((), ())), preferred_element_type=F32
    )


def gelu_pair(values):
    cdf = 0.5 + 0.5 * lax.erf(values * math.sqrt(0.5))
    pdf = jnp.exp2(values * values * (-0.5 * math.log2(math.e))) * (1.0 / math.sqrt(2.0 * math.pi))
    return (values * cdf, cdf + values * pdf)


@functools.lru_cache(maxsize=None)
def lon_matrix():
    slots = LON // 2
    points = np.arange(LON)
    table = np.zeros((slots, 2, LON))
    for slot in range(slots):
        angles = 2.0 * np.pi * (slot * points % LON) / LON
        table[slot, 0] = np.cos(angles)
        table[slot, 1] = -np.sin(angles)
    table[0, 1] = np.where(points % 2 == 0, 1.0, -1.0)
    table /= np.sqrt(LON)
    full = np.zeros((slots, 2, GROUP, GROUP, LON))
    for row in range(GROUP):
        full[:, :, row, row, :] = table
    return full.reshape(slots * 2 * GROUP, GROUP * LON)


@functools.lru_cache(maxsize=None)
def lat_matrices(parts):
    per_part = LAT // parts
    groups = per_part // GROUP
    forward = np.zeros((2, 2, ROWS, LAT, 2, 2))
    share = np.zeros((2, ROWS))
    lat = np.arange(LAT)

    def put_plain(variant, start, slot):
        for mode in range(LAT):
            angles = 2.0 * np.pi * (mode * lat % LAT) / LAT
            forward[variant, 0, start + mode, :, slot, 0] = np.cos(angles)
            forward[variant, 0, start + mode, :, slot, 1] = np.sin(angles)
            forward[variant, 1, start + mode, :, slot, 0] = -np.sin(angles)
            forward[variant, 1, start + mode, :, slot, 1] = np.cos(angles)
            share[variant, start + mode] = 1.0

    half = LAT // 2 + 1
    for column in range(2):
        for mode in range(half):
            angles = 2.0 * np.pi * (mode * lat % LAT) / LAT
            row = column * half + mode
            own = mode in (0, LAT // 2)
            forward[0, 0, row, :, 0, column] = np.cos(angles)
            forward[0, 1, row, :, 0, column] = 0.0 if own else -np.sin(angles)
            share[0, row] = 0.5 if own else 1.0
    put_plain(0, 2 * half, 1)
    put_plain(1, 0, 0)
    put_plain(1, LAT, 1)
    forward /= np.sqrt(LAT)
    forward = forward.reshape(2, 2, ROWS, parts, groups, GROUP, 2, 2)
    forward = forward.transpose(0, 1, 2, 3, 4, 6, 7, 5)
    shift_row = np.zeros((2, ROWS, 128))
    shift_row[0, 0] = np.sqrt(LAT * LON)
    return (forward, share, shift_row)


def lat_tables(parts):
    forward, share, shift_row = lat_matrices(parts)
    tall = 2 * ROWS
    wide = forward[0].size // tall
    by_part = forward.reshape(2, tall, wide)
    by_group = forward.transpose(0, 1, 2, 4, 3, 5, 6, 7).reshape(2, tall, wide)
    weights = np.concatenate([share, share], axis=1)[:, :, None]
    tables = (
        by_part,
        (weights * by_group).transpose(0, 2, 1),
        weights * by_group,
        by_part.transpose(0, 2, 1),
    )
    return tuple(jnp.asarray(table, BF16) for table in tables) + (jnp.asarray(shift_row, F32),)


def normalise(values):
    center = values - jnp.mean(values, axis=-1, keepdims=True)
    inv_std = lax.rsqrt(jnp.mean(center * center, axis=-1, keepdims=True) + NORM_EPS)
    return (center * inv_std, inv_std)


def spread_body(tokens_ref, table_ref, filter_ref, small_ref, low_ref, high_ref):
    step = pl.program_id(0)
    values = tokens_ref[...].astype(F32).reshape(GROUP * LON, 2 * HALF)
    normed, _ = normalise(values)
    out = dot(table_ref[...], normed.astype(BF16), 1, 0).astype(BF16)
    pairs = high_ref.shape[1]
    parts = high_ref.shape[0]
    units = low_ref.shape[1]
    low_ref[:, pl.ds(step * pairs, pairs)] = out[:, :HALF].reshape(parts, pairs, 16, HALF)
    high_ref[...] = out[:, HALF:].reshape(parts, pairs, 16, HALF)

    @pl.when(step == 0)
    def _():
        rows = filter_ref.shape[0]
        extra = units - pl.num_programs(0) * pairs
        spare = jnp.zeros((16 * extra - rows - 1, HALF), F32)
        own = jnp.concatenate([filter_ref[...], small_ref[...], spare], axis=0).astype(BF16)
        own = own.reshape(1, extra, 16, HALF)
        low_ref[:, units - extra :] = jnp.broadcast_to(own, (parts, extra, 16, HALF))


def spread(tokens, table, filter_rows, small_row, parts):
    groups = tokens.shape[1] // GROUP
    pairs = LON // 4 // parts
    extra = filter_rows.shape[0] // 16 + 1
    low = (parts, groups * pairs + extra, 16, HALF)
    high = (parts, groups * pairs, 16, HALF)

    def whole(*shape):
        return pl.BlockSpec(shape, lambda r: (0,) * len(shape))

    return pl.pallas_call(
        spread_body,
        name="norm_and_longitude",
        grid=(groups,),
        in_specs=[
            pl.BlockSpec((1, GROUP, LON, 2 * HALF), lambda r: (0, r, 0, 0)),
            whole(*table.shape),
            whole(*filter_rows.shape),
            whole(*small_row.shape),
        ],
        out_specs=[
            whole(*low),
            pl.BlockSpec((parts, pairs, 16, HALF), lambda r: (0, r, 0, 0)),
        ],
        out_shape=[jax.ShapeDtypeStruct(low, BF16), jax.ShapeDtypeStruct(high, BF16)],
        compiler_params=SCHED,
        cost_estimate=cost(7, 2 * tokens.size),
    )(tokens, table, filter_rows, small_row)


def unit_specs(parts, groups, pairs):
    return [
        pl.BlockSpec((parts, 1, 16, HALF), lambda b, pick_ref, r=r: (0, r * pairs + b, 0, 0))
        for r in range(groups)
    ]


def stacked(refs):
    return jnp.concatenate([ref[...] for ref in refs], axis=1).reshape(-1, HALF)


def filter_body(
    pieces,
    pick_ref,
    *refs,
):
    arrived_refs = refs[: sum(pieces)]
    forward_ref, inverse_ref, shift_row_ref, params_ref, one_ref, two_ref, *outs = refs[
        sum(pieces) :
    ]
    back_refs = outs[:-3]
    modes_ref, sums_ref, slopes_ref = outs[-3:]
    columns = forward_ref.shape[-1]
    raw = dot(forward_ref[0], stacked(arrived_refs), 1, 0)
    gain = params_ref[0:1, :]
    shift = params_ref[1:2, :]
    modes_re = (raw[:ROWS] * gain + shift_row_ref[0, :, 0:1] * shift).astype(BF16)
    modes_im = (raw[ROWS:] * gain).astype(BF16)
    modes_ref[0, :ROWS] = modes_re
    modes_ref[0, ROWS:] = modes_im
    from_re = dot(modes_re, one_ref[0], 1, 0)
    from_im = dot(modes_im, one_ref[0], 1, 0)
    bias_re = params_ref[4:5, :]
    bias_im = params_ref[5:6, :]
    re_a = from_re[:, :HALF] + bias_re
    re_b = from_re[:, HALF:] + bias_im
    im_a = from_im[:, :HALF]
    im_b = from_im[:, HALF:]
    plus_re, slope = gelu_pair(re_a - im_b)
    slopes_ref[0, 0] = slope.astype(BF16)
    minus_re, slope = gelu_pair(re_a + im_b)
    slopes_ref[0, 1] = slope.astype(BF16)
    sums_ref[0, 0, :, :HALF] = (plus_re + minus_re).astype(BF16)
    sums_ref[0, 1, :, HALF:] = (plus_re - minus_re).astype(BF16)
    plus_im, slope = gelu_pair(re_b + im_a)
    slopes_ref[0, 2] = slope.astype(BF16)
    minus_im, slope = gelu_pair(re_b - im_a)
    slopes_ref[0, 3] = slope.astype(BF16)
    sums_ref[0, 0, :, HALF:] = (-plus_im - minus_im).astype(BF16)
    sums_ref[0, 1, :, :HALF] = (plus_im - minus_im).astype(BF16)
    two_bias_re = params_ref[6:7, :]
    two_bias_im = params_ref[7:8, :]
    two_re = dot(sums_ref[0, 0], two_ref[0], 1, 0) + (two_bias_re + two_bias_re)
    two_im = dot(sums_ref[0, 1], two_ref[0], 1, 0) + (two_bias_im - two_bias_im)
    both = jnp.concatenate([two_re.astype(BF16), two_im.astype(BF16)], axis=0)
    back = dot(inverse_ref[0], both, 1, 0).astype(BF16)
    step = columns // sum(pieces)
    group = 0
    for ref, count in zip(back_refs, pieces):
        for place in range(count):
            rows = back[group * step : (group + 1) * step]
            ref[:, place] = rows.reshape(-1, 1, 16, HALF)
            group += 1


def filter_forward(pick, arrived, tables, params, one, two, part_of_channels, pieces):
    parts = arrived.shape[0]
    groups = sum(pieces)
    pairs = LON // 4 // parts
    forward, inverse, _, _, shift_row = tables
    q = part_of_channels
    tall = 2 * ROWS

    def chosen(*shape):
        return pl.BlockSpec((1,) + shape, lambda b, pick_ref: (pick_ref[b], 0, 0))

    def fixed(*shape):
        return pl.BlockSpec((1,) + shape, lambda b, pick_ref: (q, 0, 0))

    def stepped(*shape):
        zeros = (0,) * len(shape)
        return pl.BlockSpec((1,) + shape, lambda b, pick_ref: (b,) + zeros)

    back_blocks = [
        pl.BlockSpec((parts, count, 1, 16, HALF), lambda b, pick_ref: (0, 0, b, 0, 0))
        for count in pieces
    ]
    back_shapes = [jax.ShapeDtypeStruct((parts, count, pairs, 16, HALF), BF16) for count in pieces]
    columns = forward.shape[-1]
    return pl.pallas_call(
        functools.partial(filter_body, pieces),
        name="filter_forward",
        grid_spec=pltpu.PrefetchScalarGridSpec(
            num_scalar_prefetch=1,
            grid=(pairs,),
            in_specs=unit_specs(parts, groups, pairs)
            + [
                chosen(tall, columns),
                chosen(columns, tall),
                chosen(ROWS, 128),
                pl.BlockSpec((16, HALF), lambda b, pick_ref: (0, q)),
                fixed(HALF, 2 * HALF),
                fixed(2 * HALF, HALF),
            ],
            out_specs=back_blocks
            + [stepped(tall, HALF), stepped(2, ROWS, 2 * HALF), stepped(4, ROWS, HALF)],
        ),
        out_shape=back_shapes
        + [
            jax.ShapeDtypeStruct((pairs, tall, HALF), BF16),
            jax.ShapeDtypeStruct((pairs, 2, ROWS, 2 * HALF), BF16),
            jax.ShapeDtypeStruct((pairs, 4, ROWS, HALF), BF16),
        ],
        compiler_params=SCHED,
        cost_estimate=cost(14, 12 * 1024 * 1024),
    )(pick, *[arrived] * groups, forward, inverse, shift_row, params, one, two)


def filter_back_body(
    groups,
    pick_ref,
    *refs,
):
    arrived_refs = refs[:groups]
    adjoint_ref, inverse_ref, shift_row_ref, one_ref, two_ref = refs[groups : groups + 5]
    normed_refs = refs[groups + 5 : 2 * groups + 5]
    modes_ref, sums_ref, slopes_ref = refs[2 * groups + 5 : 2 * groups + 8]
    sent_ref, one_grad_ref, two_grad_ref, bias_ref = refs[2 * groups + 8 :]
    columns = adjoint_ref.shape[-1]
    step = columns // groups
    arrived = jnp.concatenate([ref[...].reshape(step, HALF) for ref in arrived_refs], axis=0)
    grad = dot(adjoint_ref[0], arrived, 1, 0)
    grad_re = grad[:ROWS].astype(BF16)
    grad_im = grad[ROWS:].astype(BF16)
    from_re = dot(grad_re, two_ref[0], 1, 1)
    from_im = dot(grad_im, two_ref[0], 1, 1)
    du = from_re[:, :HALF]
    dv = -from_re[:, HALF:]
    dw = from_im[:, :HALF]
    dx = from_im[:, HALF:]
    plus_re = (du + dx) * slopes_ref[0, 0].astype(F32)
    minus_re = (du - dx) * slopes_ref[0, 1].astype(F32)
    plus_im = (dv + dw) * slopes_ref[0, 2].astype(F32)
    minus_im = (dv - dw) * slopes_ref[0, 3].astype(F32)
    re_a = plus_re + minus_re
    im_b = minus_re - plus_re
    im_a = plus_im - minus_im
    re_b = plus_im + minus_im
    out_re = jnp.concatenate([re_a.astype(BF16), re_b.astype(BF16)], axis=1)
    out_im = jnp.concatenate([im_a.astype(BF16), im_b.astype(BF16)], axis=1)
    modes_re = dot(out_re, one_ref[0], 1, 1)
    modes_im = dot(out_im, one_ref[0], 1, 1)
    both = jnp.concatenate([modes_re.astype(BF16), modes_im.astype(BF16)], axis=0)
    sent = dot(inverse_ref[0], both, 1, 0).astype(BF16)
    sent_ref[...] = sent.reshape(sent_ref.shape)
    one_part = dot(modes_ref[0, :ROWS], out_re, 0, 0) + dot(modes_ref[0, ROWS:], out_im, 0, 0)
    two_part = dot(sums_ref[0, 0], grad_re, 0, 0) + dot(sums_ref[0, 1], grad_im, 0, 0)
    gain_part = sent.astype(F32) * stacked(normed_refs).astype(F32)
    shift_part = modes_re * shift_row_ref[0, :, 0:1]
    rows = [
        jnp.sum(part, axis=0, keepdims=True)
        for part in (re_a, re_b, grad[:ROWS], grad[ROWS:], gain_part, shift_part)
    ]
    bias_part = jnp.concatenate(rows + [jnp.zeros((2, HALF), F32)], axis=0)
    first = pl.program_id(0) == 0

    @pl.when(first)
    def _():
        one_grad_ref[...] = one_part
        two_grad_ref[...] = two_part
        bias_ref[...] = bias_part

    @pl.when(jnp.logical_not(first))
    def _():
        one_grad_ref[...] += one_part
        two_grad_ref[...] += two_part
        bias_ref[...] += bias_part


def filter_backward(pick, arrived, tables, one, two, normed, modes, sums, slopes, part_of_channels):
    groups = len(arrived)
    parts, pairs = arrived[0].shape[:2]
    _, _, adjoint, inverse, shift_row = tables
    q = part_of_channels
    tall = 2 * ROWS
    columns = adjoint.shape[-1]

    def chosen(*shape):
        return pl.BlockSpec((1,) + shape, lambda b, pick_ref: (pick_ref[b], 0, 0))

    def fixed(*shape):
        return pl.BlockSpec((1,) + shape, lambda b, pick_ref: (q, 0, 0))

    def stepped(*shape):
        zeros = (0,) * len(shape)
        return pl.BlockSpec((1,) + shape, lambda b, pick_ref: (b,) + zeros)

    def whole(*shape):
        return pl.BlockSpec(shape, lambda b, pick_ref: (0,) * len(shape))

    arrived_block = pl.BlockSpec((parts, 1, 16, HALF), lambda b, pick_ref: (0, b, 0, q))
    return pl.pallas_call(
        functools.partial(filter_back_body, groups),
        name="filter_backward",
        grid_spec=pltpu.PrefetchScalarGridSpec(
            num_scalar_prefetch=1,
            grid=(pairs,),
            in_specs=[arrived_block] * groups
            + [
                chosen(tall, columns),
                chosen(columns, tall),
                chosen(ROWS, 128),
                fixed(HALF, 2 * HALF),
                fixed(2 * HALF, HALF),
            ]
            + unit_specs(parts, groups, pairs)
            + [
                stepped(tall, HALF),
                stepped(2, ROWS, 2 * HALF),
                stepped(4, ROWS, HALF),
            ],
            out_specs=[
                pl.BlockSpec((parts, groups, 1, 16, HALF), lambda b, pick_ref: (0, 0, b, 0, 0)),
                whole(HALF, 2 * HALF),
                whole(2 * HALF, HALF),
                whole(8, HALF),
            ],
        ),
        out_shape=[
            jax.ShapeDtypeStruct((parts, groups, pairs, 16, HALF), BF16),
            jax.ShapeDtypeStruct((HALF, 2 * HALF), F32),
            jax.ShapeDtypeStruct((2 * HALF, HALF), F32),
            jax.ShapeDtypeStruct((8, HALF), F32),
        ],
        compiler_params=SCHED,
        cost_estimate=cost(18, 12 * 1024 * 1024),
    )(pick, *arrived, adjoint, inverse, shift_row, one, two, *[normed] * groups, modes, sums, slopes)


def dense_body(
    tokens_ref,
    cotangent_ref,
    low_ref,
    high_ref,
    inverse_ref,
    table_ref,
    params_ref,
    in_bias_ref,
    in_ref,
    out_ref,
    *refs,
):
    (
        result_ref,
        mixed_grad_ref,
        second_ref,
        grad_low_ref,
        act_ref,
        grad_pre_ref,
        sent_ref,
        in_bias_grad_ref,
        rows_ref,
        branch_ref,
        grad_second_ref,
        normed_two_ref,
        inv_two_ref,
        normed_one_ref,
    ) = refs[-14:]
    chunk = pl.program_id(0)
    count = GROUP * LON
    wide = 2 * HALF

    @pl.when(chunk == 0)
    def _():
        inputs = tokens_ref[...].astype(F32).reshape(count, wide)
        normed, _ = normalise(inputs)
        normed_one_ref[...] = normed.astype(BF16)
        base = normed * params_ref[0:1, :] + params_ref[1:2, :] + inputs
        arrived = jnp.concatenate(
            [low_ref[...].reshape(count, HALF), high_ref[...].reshape(count, HALF)], axis=1
        )
        mixed = dot(inverse_ref[...], arrived, 1, 0) + base
        branch_ref[...] = mixed + params_ref[8:9, :]
        normed_two, inv_two = normalise(mixed)
        normed_two_ref[...] = normed_two
        inv_two_ref[...] = jnp.broadcast_to(inv_two, inv_two_ref.shape)
        second_ref[...] = (normed_two * params_ref[2:3, :] + params_ref[3:4, :]).astype(BF16)
        grad_low_ref[...] = (
            cotangent_ref[...].astype(F32).reshape(count, wide) * params_ref[13:14, :]
        ).astype(BF16)
        grad_second_ref[...] = jnp.zeros_like(grad_second_ref)

    pre = dot(second_ref[...], in_ref[...], 1, 0) + in_bias_ref[...]
    grad_act = dot(grad_low_ref[...], out_ref[...], 1, 1)
    act, slope = gelu_pair(pre)
    act = act.astype(BF16)
    grad_pre = grad_act * slope
    in_bias_grad_ref[...] = jnp.sum(grad_pre, axis=0, keepdims=True)
    grad_pre = grad_pre.astype(BF16)
    act_ref[...] = act
    grad_pre_ref[...] = grad_pre
    branch_ref[...] += dot(act, out_ref[...], 1, 0)
    grad_second_ref[...] += dot(grad_pre, in_ref[...], 1, 1)

    @pl.when(chunk == pl.num_programs(0) - 1)
    def _():
        result_ref[...] = branch_ref[...].astype(BF16).reshape(result_ref.shape)
        normed_two = normed_two_ref[...]
        inv_two = inv_two_ref[:, 0:1]
        upstream = grad_second_ref[...]
        scaled = upstream * params_ref[2:3, :]
        first_mean = jnp.mean(scaled, axis=-1, keepdims=True)
        second_mean = jnp.mean(scaled * normed_two, axis=-1, keepdims=True)
        grad_out = cotangent_ref[...].astype(F32).reshape(count, wide) * params_ref[13:14, :]
        mixed_grad = grad_out + inv_two * (scaled - first_mean - normed_two * second_mean)
        mixed_grad_ref[...] = mixed_grad.astype(BF16).reshape(mixed_grad_ref.shape)
        rows = [
            jnp.sum(part, axis=0, keepdims=True)
            for part in (upstream * normed_two, upstream, grad_low_ref[...].astype(F32))
        ]
        normed_one = normed_one_ref[...].astype(F32)
        rows += [
            jnp.sum(part, axis=0, keepdims=True) for part in (mixed_grad * normed_one, mixed_grad)
        ]
        rows_ref[...] = jnp.concatenate(rows + [jnp.zeros((3, wide), F32)], axis=0)
        sent = dot(table_ref[...], mixed_grad.astype(BF16), 1, 0).astype(BF16)
        sent_ref[...] = sent.reshape(sent_ref.shape)


def dense(
    kept, tokens, cotangent, low, high, places, inverse, table, params, in_bias, in_work, out_work, group
):
    parts, _, pairs = high.shape[:3]
    groups = tokens.shape[1] // GROUP
    count = GROUP * LON
    wide = 2 * HALF
    hidden = in_work.shape[1]

    def whole(*shape):
        return pl.BlockSpec(shape, lambda f: (0,) * len(shape))

    rows = pl.BlockSpec((1, GROUP, LON, wide), lambda f: (0, group, 0, 0))
    low_spec, high_spec = (
        pl.BlockSpec((parts, 1, pairs, 16, HALF), lambda f, place=place: (0, place, 0, 0, 0))
        for place in places
    )
    token_rows = pl.BlockSpec((count, wide), lambda f: (group, 0))
    hidden_rows = pl.BlockSpec((count, FCHUNK), lambda f: (group, f))
    return pl.pallas_call(
        dense_body,
        name="dense_group",
        grid=(hidden // FCHUNK,),
        in_specs=[
            rows,
            rows,
            low_spec,
            high_spec,
            whole(*inverse.shape),
            whole(*table.shape),
            whole(16, wide),
            pl.BlockSpec((1, FCHUNK), lambda f: (0, f)),
            pl.BlockSpec((wide, FCHUNK), lambda f: (0, f)),
            pl.BlockSpec((FCHUNK, wide), lambda f: (f, 0)),
        ]
        + [pl.BlockSpec(memory_space=pl.ANY)] * len(kept),
        out_specs=[
            rows,
            rows,
            token_rows,
            token_rows,
            hidden_rows,
            hidden_rows,
            whole(parts, pairs, 16, wide),
            pl.BlockSpec((1, FCHUNK), lambda f: (0, f)),
            whole(8, wide),
        ],
        out_shape=[
            jax.ShapeDtypeStruct(tokens.shape, BF16),
            jax.ShapeDtypeStruct(tokens.shape, BF16),
            jax.ShapeDtypeStruct((groups * count, wide), BF16),
            jax.ShapeDtypeStruct((groups * count, wide), BF16),
            jax.ShapeDtypeStruct((groups * count, hidden), BF16),
            jax.ShapeDtypeStruct((groups * count, hidden), BF16),
            jax.ShapeDtypeStruct((parts, pairs, 16, wide), BF16),
            jax.ShapeDtypeStruct((1, hidden), F32),
            jax.ShapeDtypeStruct((8, wide), F32),
        ],
        scratch_shapes=[pltpu.VMEM((count, wide), F32)] * 3
        + [pltpu.VMEM((count, 128), F32), pltpu.VMEM((count, wide), BF16)],
        input_output_aliases={10 + i: i for i in range(len(kept))},
        compiler_params=SCHED,
        cost_estimate=cost(25, 30 * 1024 * 1024),
    )(tokens, cotangent, low, high, inverse, table, params, in_bias, in_work, out_work, *kept)


def gather_grad_body(
    tokens_ref, mixed_grad_ref, low_ref, high_ref, inverse_ref, params_ref, grad_ref
):
    count = GROUP * LON
    wide = 2 * HALF
    mixed_grad = mixed_grad_ref[...].astype(F32).reshape(count, wide)
    low = dot(inverse_ref[...], low_ref[...].reshape(count, HALF), 1, 0)
    high = dot(inverse_ref[...], high_ref[...].reshape(count, HALF), 1, 0)
    upstream = mixed_grad + jnp.concatenate([low, high], axis=1)
    normed, inv_std = normalise(tokens_ref[...].astype(F32).reshape(count, wide))
    scaled = upstream * params_ref[0:1, :]
    first_mean = jnp.mean(scaled, axis=-1, keepdims=True)
    second_mean = jnp.mean(scaled * normed, axis=-1, keepdims=True)
    out = mixed_grad + inv_std * (scaled - first_mean - normed * second_mean)
    grad_ref[...] = out.reshape(grad_ref.shape)


def gather_grad(tokens, mixed_grad, low, high, inverse, params):
    parts, groups, pairs = low.shape[:3]
    wide = 2 * HALF

    def whole(*shape):
        return pl.BlockSpec(shape, lambda r: (0,) * len(shape))

    rows = pl.BlockSpec((1, GROUP, LON, wide), lambda r: (0, r, 0, 0))
    arrived = pl.BlockSpec((parts, 1, pairs, 16, HALF), lambda r: (0, r, 0, 0, 0))
    return pl.pallas_call(
        gather_grad_body,
        name="longitude_and_norm_grad",
        grid=(groups,),
        in_specs=[rows, rows, arrived, arrived, whole(*inverse.shape), whole(16, wide)],
        out_specs=rows,
        out_shape=jax.ShapeDtypeStruct((1, groups * GROUP, LON, wide), F32),
        compiler_params=SCHED,
        cost_estimate=cost(12, 16 * 1024 * 1024),
    )(tokens, mixed_grad, low, high, inverse, params)


def block_matrices(weight):
    size = weight.shape[1] // 4
    places = np.arange(HALF)
    pick = (np.arange(4 * size)[:, None, None] == np.arange(4)[:, None] * size + places % size)
    own = places[:, None] // size == places[None, :] // size
    halves = weight.reshape(2, HALF, 4 * size)

    def spread_columns(form, first):
        full = jnp.einsum(
            form, halves, jnp.asarray(pick[:, first : first + 2], BF16), preferred_element_type=F32
        )
        return full

    one = spread_columns("qrc,cpn->qrpn", 0) * own[:, None, :]
    two = spread_columns("qrc,cpn->qprn", 2) * own
    return (
        one.astype(BF16).reshape(2, HALF, 2 * HALF),
        two.astype(BF16).reshape(2, 2 * HALF, HALF),
    )


def own_blocks(matrix, size):
    count = HALF // size
    return jnp.concatenate(
        [matrix[i * size : (i + 1) * size, i * size : (i + 1) * size] for i in range(count)], axis=0
    )


def in_turn(values, last):
    return lax.optimization_barrier((values, last))[0]


def exchange(values, last=None):
    if last is not None:
        values = in_turn(values, last)
    return lax.all_to_all(values, "sp", split_axis=0, concat_axis=0, tiled=True)


AXES = ("y", "core", "sp")
BITS = (("y", 1), ("core", 1), ("sp", 4), ("sp", 2), ("sp", 1))
SIZES = {"y": 2, "core": 2, "sp": 8}


def swap(values, axis, bit):
    return lax.ppermute(values, axis, [(i, i ^ bit) for i in range(SIZES[axis])])


def mine(axis, bit):
    return (lax.axis_index(axis) // bit) % 2


def gather_bit(values, axis, bit, place=0, last=None):
    other = swap(values, axis, bit)
    if last is not None:
        other = in_turn(other, last)
    low = mine(axis, bit) == 0
    return jnp.stack([jnp.where(low, values, other), jnp.where(low, other, values)], axis=place)


def gather_steps(values, held, order, last=None):
    for axis, bit in order:
        held = sorted([*held, (axis, bit)], key=BITS.index)
        values = gather_bit(values, axis, bit, held.index((axis, bit)), last)
    return values, held


def scatter_small(values, last):
    held = list(BITS)
    values = values.reshape((2,) * len(held) + values.shape[1:])
    for step, (axis, bit) in enumerate(IN_ORDER):
        if step == 3:
            values = in_turn(values, last)
        place = held.index((axis, bit))
        keep = lax.dynamic_index_in_dim(values, mine(axis, bit), place, keepdims=False)
        give = lax.dynamic_index_in_dim(values, 1 - mine(axis, bit), place, keepdims=False)
        values = keep + swap(give, axis, bit)
        held.pop(place)
    return values


SMALL = pl.CostEstimate(flops=1 << 20, bytes_accessed=1 << 20, transcendentals=0)
IN_ORDER = (("core", 1), ("y", 1), ("sp", 1), ("sp", 2), ("sp", 4))
OUT_ORDER = (("core", 1), ("sp", 1), ("y", 1), ("sp", 2), ("sp", 4))


def device_rows(order):
    lists = []
    for core in range(2):
        indices = []
        for count in range(16):
            samp, sp = core, 0
            for place, (axis, bit) in enumerate(order[1:]):
                if count >> (3 - place) & 1:
                    samp, sp = (samp + 2 * bit, sp) if axis == "y" else (samp, sp + bit)
            indices.append(samp * 8 + sp)
        lists.append(indices)
    return lists


def in_weight_grad_body(pick_ref, second_ref, grad_pre_ref, keep_ref, give_ref):
    out = dot(second_ref[...], grad_pre_ref[...], 0, 0)
    rows = out.shape[0] // 32
    halves = [
        jnp.concatenate([out[i * rows : (i + 1) * rows] for i in indices], axis=0).astype(BF16)
        for indices in device_rows(IN_ORDER)
    ]

    @pl.when(pick_ref[0] == 0)
    def _():
        keep_ref[...] = halves[0]
        give_ref[...] = halves[1]

    @pl.when(pick_ref[0] == 1)
    def _():
        keep_ref[...] = halves[1]
        give_ref[...] = halves[0]


def in_weight_grad(core, second, grad_pre):
    tokens, wide = second.shape
    hidden = grad_pre.shape[1]
    step = 512
    half = pl.BlockSpec((wide // 2, step), lambda i, pick_ref: (0, i))
    return pl.pallas_call(
        in_weight_grad_body,
        name="in_weight_grad",
        grid_spec=pltpu.PrefetchScalarGridSpec(
            num_scalar_prefetch=1,
            grid=(hidden // step,),
            in_specs=[
                pl.BlockSpec((tokens, wide), lambda i, pick_ref: (0, 0)),
                pl.BlockSpec((tokens, step), lambda i, pick_ref: (0, i)),
            ],
            out_specs=[half, half],
        ),
        out_shape=[jax.ShapeDtypeStruct((wide // 2, hidden), BF16)] * 2,
        compiler_params=SCHED,
        cost_estimate=SMALL,
    )(core, second, grad_pre)


def out_weight_grad_body(pick_ref, act_ref, grad_low_ref, keep_ref, give_ref):
    out = dot(act_ref[...], grad_low_ref[...], 0, 0)
    rows = out.shape[0] // 8
    out = out.astype(BF16)
    pieces = [
        jnp.concatenate(
            [
                out[(z1 * 4 + z0 * 2 + x) * rows : (z1 * 4 + z0 * 2 + x + 1) * rows]
                for z0 in range(2)
                for z1 in range(2)
            ],
            axis=0,
        )
        for x in range(2)
    ]

    @pl.when(pl.program_id(0) == 0)
    def _():
        for x in range(2):
            keep_ref[x, 0] = pieces[x]

    @pl.when(pl.program_id(0) == 1)
    def _():
        for x in range(2):
            give_ref[x, 0] = pieces[x]


def out_weight_grad(core, act, grad_low):
    tokens, hidden = act.shape
    wide = grad_low.shape[1]
    part = hidden // 4
    shape = (2, 2, part // 2, wide)

    def columns(give, y, pick_ref):
        return (0, y * 2 + (pick_ref[0] + give) % 2)

    keep, give = pl.pallas_call(
        out_weight_grad_body,
        name="out_weight_grad",
        grid_spec=pltpu.PrefetchScalarGridSpec(
            num_scalar_prefetch=1,
            grid=(2, 2),
            in_specs=[
                pl.BlockSpec((tokens, part), columns),
                pl.BlockSpec((tokens, wide), lambda give, y, pick_ref: (0, 0)),
            ],
            out_specs=[
                pl.BlockSpec(
                    (2, 1) + shape[2:], lambda give, y, pick_ref: (0, jnp.maximum(y, give), 0, 0)
                ),
                pl.BlockSpec((2, 1) + shape[2:], lambda give, y, pick_ref: (0, y * give, 0, 0)),
            ],
        ),
        out_shape=[jax.ShapeDtypeStruct(shape, BF16)] * 2,
        compiler_params=SCHED,
        cost_estimate=SMALL,
    )(core, act, grad_low)
    return keep.reshape(-1, wide), give.reshape(-1, wide)


def add_split_body(pick_ref, keep_one, got_one, keep_two, got_two, keep_ref, give_ref):
    keep_ref[...] = (keep_one[...].astype(F32) + got_one[...].astype(F32)).astype(BF16)
    give_ref[...] = (keep_two[...].astype(F32) + got_two[...].astype(F32)).astype(BF16)


def add_split(pick, keep, got):
    rows, columns = keep.shape
    steps = 2 if rows % 64 == 0 else 1
    block = (rows // 2 // steps, columns)
    stays = pl.BlockSpec(block, lambda i, pick_ref: (pick_ref[0] * steps + i, 0))
    goes = pl.BlockSpec(block, lambda i, pick_ref: ((1 - pick_ref[0]) * steps + i, 0))
    out = pl.BlockSpec(block, lambda i, pick_ref: (i, 0))
    return pl.pallas_call(
        add_split_body,
        name="add_split",
        grid_spec=pltpu.PrefetchScalarGridSpec(
            num_scalar_prefetch=1,
            grid=(steps,),
            in_specs=[stays, stays, goes, goes],
            out_specs=[out, out],
        ),
        out_shape=[jax.ShapeDtypeStruct((rows // 2, columns), BF16)] * 2,
        compiler_params=SCHED,
        cost_estimate=SMALL,
    )(pick, keep, got, keep, got)


def picks(order):
    return [mine(axis, bit).astype(jnp.int32).reshape(1) for axis, bit in order]


def scatter_steps(keep, give, order, chosen, first, last):
    for place in range(first, last):
        keep, give = add_split(chosen[place + 1], keep, swap(give, *order[place]))
    return keep, give


def scatter_last(keep, give, order):
    return keep.astype(F32) + swap(give, *order[-1]).astype(F32)


def fast_shards(
    sizes,
    tokens,
    cotangent,
    storm_weight,
    filter_master,
    in_master,
    out_master,
    small_master,
    filter_m,
    filter_v,
    in_m,
    in_v,
    out_m,
    out_v,
    small_m,
    small_v,
    filter_ema,
    in_ema,
    out_ema,
    small_ema,
):
    parts = sizes[1]
    devices = sizes[0] * sizes[1]
    groups = tokens.shape[1] // GROUP
    pairs = LON // 4 // parts
    width = tokens.shape[-1]
    block = width // NB
    small_share = small_master.shape[0]
    sp_index = lax.axis_index("sp")

    lon = lon_matrix()
    lon_table = jnp.asarray(lon, BF16)
    lon_back = jnp.asarray(lon.T, BF16)
    tables = lat_tables(parts)
    pick = jnp.where((sp_index == 0) & (jnp.arange(pairs) == 0), 0, 1).astype(jnp.int32)

    filter_rows = filter_master.shape[0]
    small_row = jnp.pad(small_master, (0, 4 * block - small_share)).reshape(1, -1)
    in_gather, out_gather = IN_ORDER[::-1], IN_ORDER[::-1]
    in_part, in_held = gather_steps(in_master.astype(BF16), [], in_gather[:1])
    out_part, out_held = gather_steps(out_master.astype(BF16), [], out_gather[:1])
    sent = spread(tokens, lon_table, filter_master, small_row, parts)
    arrived_low = exchange(sent[0], (in_part, out_part))
    arrived_high = exchange(sent[1], arrived_low)

    units = groups * pairs
    near = arrived_low[:, units:].reshape(parts, -1, 4 * block)
    packed_all = gather_bit(gather_bit(near, "core", 1), "y", 1)
    packed_all = packed_all.reshape((devices,) + near.shape[1:])
    filter_work = packed_all[:, :filter_rows].reshape(width, 4 * block)
    small_work = packed_all[:, filter_rows, :small_share].reshape(-1)

    in_rows, hidden = in_master.shape
    params = small_work.astype(F32).reshape(13, width)
    scale = storm_weight.astype(F32)[0] / 64.0
    in_bias = params[9:13].reshape(1, -1)
    params = jnp.concatenate(
        [params, jnp.full((1, width), scale, F32), jnp.zeros((2, width), F32)], axis=0
    )
    one, two = block_matrices(filter_work)
    params, in_bias = lax.optimization_barrier((params, in_bias))

    in_part, in_held = gather_steps(in_part, in_held, in_gather[1:2])
    out_part, out_held = gather_steps(out_part, out_held, out_gather[1:2])
    in_part, out_part = in_turn((in_part, out_part), arrived_low)
    forward_low = filter_forward(pick, arrived_low, tables, params, one, two, 0, (groups,))
    in_part, in_held = gather_steps(in_part, in_held, in_gather[2:3], forward_low[0])
    out_part, out_held = gather_steps(out_part, out_held, out_gather[2:3], forward_low[0])
    returned_low = exchange(forward_low[0], arrived_high)
    high_pieces = (1, groups - 1) if groups > 1 else (1,)
    forward_high = filter_forward(pick, arrived_high, tables, params, one, two, 1, high_pieces)
    last = returned_low
    returned_high = []
    for piece in range(len(high_pieces)):
        last = exchange(forward_high[piece], last)
        returned_high.append(last)
    in_part, in_held = gather_steps(in_part, in_held, in_gather[3:4], returned_high[0])
    in_work = gather_steps(in_part, in_held, in_gather[4:])[0].reshape(width, hidden)
    out_part, out_held = gather_steps(out_part, out_held, out_gather[3:4], forward_high[0])
    out_work = gather_steps(out_part, out_held, out_gather[4:])[0].reshape(hidden, width)
    kept = []
    grad_arrived = []
    dense_rows = 0.0
    in_bias_grad = 0.0
    for group in range(groups):
        piece = min(group, 1)
        *kept, sent_piece, bias_piece, rows_piece = dense(
            kept,
            tokens,
            cotangent,
            returned_low,
            returned_high[piece],
            (group, group - piece),
            lon_back,
            lon_table,
            params,
            in_bias,
            in_work,
            out_work,
            group,
        )
        in_bias_grad = in_bias_grad + bias_piece
        dense_rows = dense_rows + rows_piece
        before_last = last
        last = exchange(sent_piece, last)
        grad_arrived.append(last)
    result, mixed_grad, second, grad_low, act, grad_pre = kept
    act, grad_pre = in_turn((act, grad_pre), before_last)
    in_picks, out_picks = picks(IN_ORDER), picks(OUT_ORDER)
    out_part, in_part = in_turn(
        (
            out_weight_grad(out_picks[0], act, grad_low),
            in_weight_grad(in_picks[0], second, grad_pre),
        ),
        last,
    )
    out_part = scatter_steps(*out_part, OUT_ORDER, out_picks, 0, 1)
    in_part = scatter_steps(*in_part, IN_ORDER, in_picks, 0, 1)

    backward = []
    grad_returned = []
    for q, (normed, forward) in enumerate(
        ((arrived_low, forward_low), (arrived_high, forward_high))
    ):
        if q == 1:
            grad_arrived = in_turn(grad_arrived, (in_part, out_part))
        backward.append(
            filter_backward(pick, grad_arrived, tables, one, two, normed, *forward[-3:], q)
        )
        if q == 1:
            out_part = scatter_steps(*out_part, OUT_ORDER, out_picks, 1, 2)
            in_part = scatter_steps(*in_part, IN_ORDER, in_picks, 1, 2)
            last = (last, out_part, in_part)
            second_half = last
        last = exchange(backward[q][0], last)
        grad_returned.append(last)

    out_part = scatter_steps(*out_part, OUT_ORDER, out_picks, 2, 3)
    in_part = scatter_steps(*in_part, IN_ORDER, in_picks, 2, 3)
    out_part = scatter_steps(*out_part, OUT_ORDER, out_picks, 3, 4)
    in_part = scatter_steps(*in_part, IN_ORDER, in_picks, 3, 4)
    out_part, in_part = in_turn((out_part, in_part), last)
    out_grad = scatter_last(*out_part, OUT_ORDER)
    in_grad = scatter_last(*in_part, IN_ORDER)

    pieces = []
    for q in range(2):
        one_grad, two_grad = in_turn((backward[q][1], backward[q][2]), second_half)
        pieces.append(
            jnp.concatenate(
                [
                    own_blocks(one_grad[:, :HALF], block),
                    own_blocks(one_grad[:, HALF:], block),
                    own_blocks(two_grad[:HALF], block),
                    own_blocks(two_grad[HALF:], block),
                ],
                axis=1,
            )
        )
    filter_local = jnp.concatenate(pieces, axis=0).reshape(devices, filter_rows, 4 * block)
    bias_rows = jnp.concatenate([backward[0][3], backward[1][3]], axis=1)
    small_rows = jnp.concatenate(
        [
            dense_rows[3:5] + bias_rows[4:6],
            dense_rows[0:2],
            bias_rows[0:2],
            bias_rows[2:3] + bias_rows[2:3],
            bias_rows[3:4] - bias_rows[3:4],
            dense_rows[2:3],
            in_bias_grad.reshape(4, width),
        ],
        axis=0,
    )

    def shares(rows):
        flat = rows.reshape(-1)
        flat = jnp.pad(flat, (0, devices * small_share - flat.shape[0]))
        return jnp.pad(flat.reshape(devices, small_share), ((0, 0), (0, 4 * block - small_share)))

    early = scatter_small(
        jnp.concatenate([filter_local, shares(small_rows)[:, None]], axis=1), last
    )
    filter_grad = early[:filter_rows]
    small_grad = early[filter_rows, :small_share]

    input_grad = gather_grad(
        tokens,
        mixed_grad,
        grad_returned[0],
        grad_returned[1],
        lon_back,
        params,
    )

    filter_new, filter_m_new, filter_v_new, filter_ema_new = adam_update(
        filter_master, filter_grad, filter_m, filter_v, filter_ema, 0.2
    )
    in_new, in_m_new, in_v_new, in_ema_new = adam_update(
        in_master, in_grad, in_m, in_v, in_ema, 0.1
    )
    out_new, out_m_new, out_v_new, out_ema_new = adam_update(
        out_master, out_grad, out_m, out_v, out_ema, 0.05
    )
    small_new, small_m_new, small_v_new, small_ema_new = adam_update(
        small_master, small_grad, small_m, small_v, small_ema, 0.5
    )
    return (
        result,
        input_grad,
        filter_grad,
        in_grad,
        out_grad,
        small_grad,
        filter_new,
        in_new,
        out_new,
        small_new,
        filter_m_new,
        filter_v_new,
        in_m_new,
        in_v_new,
        out_m_new,
        out_v_new,
        small_m_new,
        small_v_new,
        filter_ema_new,
        in_ema_new,
        out_ema_new,
        small_ema_new,
    )


def solution(mesh):
    sizes = (mesh.shape["samp"], mesh.shape["sp"])
    samp = "samp"
    body = plain_shards
    if fits(sizes):
        samp = ("y", "core")
        mesh = Mesh(mesh.devices.reshape(2, 2, sizes[1]), AXES)
        body = functools.partial(fast_shards, sizes)
    every = (*samp, "sp") if isinstance(samp, tuple) else (samp, "sp")
    return jax.shard_map(
        body,
        mesh=mesh,
        in_specs=(
            P(samp, "sp", None, None),
            P(samp, "sp", None, None),
            P(samp),
            P(every, None),
            P(every, None),
            P(every, None),
            P(every),
            P(every, None),
            P(every, None),
            P(every, None),
            P(every, None),
            P(every, None),
            P(every, None),
            P(every),
            P(every),
            P(every, None),
            P(every, None),
            P(every, None),
            P(every),
        ),
        out_specs=(
            P(samp, "sp", None, None),
            P(samp, "sp", None, None),
            P(every, None),
            P(every, None),
            P(every, None),
            P(every),
            P(every, None),
            P(every, None),
            P(every, None),
            P(every),
            P(every, None),
            P(every, None),
            P(every, None),
            P(every, None),
            P(every, None),
            P(every, None),
            P(every),
            P(every),
            P(every, None),
            P(every, None),
            P(every, None),
            P(every),
        ),
        check_vma=False,
    )
```

profile of v0, /device:TPU:0, one launch (start us, length us, event | category | flops | bytes accessed | tf_op | source)
XLA Modules:
  0.0 468.5 jit_solution(15968814395686393080)
XLA Ops:
  1.6 4.1 collective-permute-start.1
  8.1 7.1 %norm_and_longitude.1 = (bf16[8,17,16,384]{3,2,1,0:T(8,128)(2,1)}, bf16[8,15,16,384]{3,2,1,0:T(8,128)(2,1)}) custom-call(bf16[1,12,160,768]{3,2,1,0:T(8,128)(2,1)} %tokens_ref.9, bf16[640,640]{1,0:T(8,128)(2,1)} %constant.317.clone.table_ref, f32[24,384]{1,0:T(8,128)} %filter_ref.1, f32[1,384]{1,0:T(1,128)} %reshape.123.small_ref), custom_call_target="tpu_custom_call" | custom-call | flops 8049999872 | bytes 2949120 | tf_op jit(solution)/shard_map/norm_and_longitude/pallas_call | solution.py:435
  19.1 5.8 %all-to-all-start = ((bf16[8,17,16,384]{3,2,1,0:T(8,128)(2,1)}), bf16[8,17,16,384]{3,2,1,0:T(8,128)(2,1)S(1)}, u32[]{:S(2)}, u32[]{:S(2)}) async-start(bf16[8,17,16,384]{3,2,1,0:T(8,128)(2,1)} %get-tuple-element.125), calls=%async_computation | async-start | bytes 3342336 | tf_op jit(solution)/shard_map/all_to_all | solution.py:923
  28.3 32.2 %collective-permute-done.4 = bf16[2,24,3072]{2,1,0:T(8,128)(2,1)S(1)} collective-permute-done((bf16[2,24,3072]{2,1,0:T(8,128)(2,1)S(1)}, bf16[2,24,3072]{2,1,0:T(8,128)(2,1)S(1)}, u32[]{:S(2)}, u32[]{:S(2)}) %collective-permute-start.4) | collective-permute-done | bytes 294944 | tf_op jit(solution)/shard_map/ppermute | solution.py:932
  60.5 3.8 all-to-all-done.refs_0_.refs_1_.refs_2_.refs_8_.refs_9_.refs_10_
  73.0 4.3 all-to-all-start.1
  88.1 13.8 %filter_forward.2 = (bf16[8,3,5,16,384]{4,3,2,1,0:T(8,128)(2,1)}, bf16[5,416,384]{2,1,0:T(8,128)(2,1)}, bf16[5,2,208,768]{3,2,1,0:T(8,128)(2,1)}, bf16[5,4,208,384]{3,2,1,0:T(8,128)(2,1)}) custom-call(s32[5]{0:T(128)} %and_select_fusion.pick_ref, bf16[8,17,16,384]{3,2,1,0:T(8,128)(2,1)} %copy-done.14, bf16[8,17,16,384]{3,2,1,0:T(8,128)(2,1)} %copy-done.14, ...), custom_call_target="tpu_custom_call" | custom-call | flops 16099999744 | bytes 12582912 | tf_op jit(solution)/shard_map/filter_forward/pallas_call | solution.py:544
  104.9 9.3 %collective-permute-done.6 = bf16[2,2,24,3072]{3,2,0,1:T(8,128)(2,1)} collective-permute-done((bf16[2,2,24,3072]{3,2,0,1:T(8,128)(2,1)}, bf16[2,2,24,3072]{3,2,0,1:T(8,128)(2,1)}, u32[]{:S(2)}, u32[]{:S(2)}) %collective-permute-start.6) | collective-permute-done | bytes 589856 | tf_op jit(solution)/shard_map/ppermute | solution.py:932
  114.2 4.6 all-to-all-start.2
  122.1 13.9 %filter_forward.3 = (bf16[8,1,5,16,384]{4,3,2,1,0:T(8,128)(2,1)}, bf16[8,2,5,16,384]{4,3,2,1,0:T(8,128)(2,1)}, bf16[5,416,384]{2,1,0:T(8,128)(2,1)}, bf16[5,2,20...) custom-call(s32[5]{0:T(128)} %and_select_fusion.pick_ref, ...), custom_call_target="tpu_custom_call" | custom-call | flops 16099999744 | bytes 12582912 | tf_op jit(solution)/shard_map/filter_forward/pallas_call | solution.py:544
  136.0 16.8 %all-to-all-done.2.low_ref = bf16[8,3,5,16,384]{4,3,2,1,0:T(8,128)(2,1)S(1)} async-done(((bf16[8,3,5,16,384]{4,3,2,1,0:T(8,128)(2,1)}), bf16[8,3,5,16,384]{4,3,2,1,0:T(8,128)(2,1)S(1)}, u32[]{:S(2)}, u32[]{:S(2)}) %all-to-all-start.2) | async-done | bytes 1474592 | tf_op jit(solution)/shard_map/all_to_all | solution.py:923
  152.9 4.6 all-to-all-start.3
  160.7 10.0 %all-to-all-done.3.high_ref = bf16[8,1,5,16,384]{4,3,2,1,0:T(8,128)(2,1)} async-done(((bf16[8,1,5,16,384]{4,3,2,1,0:T(8,128)(2,1)}), bf16[8,1,5,16,384]{4,3,2,1,0:T(8,128)(2,1)}, u32[]{:S(2)}, u32[]{:S(2)}) %all-to-all-start.3) | async-done | bytes 491552 | tf_op jit(solution)/shard_map/all_to_all | solution.py:923
  179.2 3.6 all-to-all-start.4
  187.9 24.2 %dense_group.3 = (bf16[1,12,160,768]{3,2,1,0:T(8,128)(2,1)}, bf16[1,12,160,768]{3,2,1,0:T(8,128)(2,1)}, bf16[1920,768]{1,0:T(8,128)(2,1)}, bf16[1920,768]{1,0:T(...) custom-call(bf16[1,12,160,768]{3,2,1,0:T(8,128)(2,1)} %tokens_ref.9,, ...), custom_call_target="tpu_custom_call" | custom-call | flops 28750000128 | bytes 31457280 | tf_op jit(solution)/shard_map/dense_group/pallas_call | solution.py:803
  213.1 6.2 %all-to-all-start.5 = ((bf16[8,5,16,768]{3,2,1,0:T(8,128)(2,1)}), bf16[8,5,16,768]{3,2,1,0:T(8,128)(2,1)S(1)}, u32[]{:S(2)}, u32[]{:S(2)}) async-start(bf16[8,5,16,768]{3,2,1,0:T(8,128)(2,1)} %get-tuple-element.157), calls=%async_computation.5 | async-start | bytes 1966080 | tf_op jit(solution)/shard_map/all_to_all | solution.py:923
  219.3 24.3 %dense_group.4 = (bf16[1,12,160,768]{3,2,1,0:T(8,128)(2,1)}, bf16[1,12,160,768]{3,2,1,0:T(8,128)(2,1)}, bf16[1920,768]{1,0:T(8,128)(2,1)}, bf16[1920,768]{1,0:T(...) custom-call(bf16[1,12,160,768]{3,2,1,0:T(8,128)(2,1)} %tokens_ref.9,, ...), custom_call_target="tpu_custom_call", output_to_operand_aliasing={{0}: (10, {}), {1}: (11, {}), {2}: (12, {}), {3}: (13, {}),... | custom-call | flops 28750000128 | bytes 31457280 | tf_op jit(solution)/shard_map/dense_group/pallas_call | solution.py:803
  243.9 5.8 %all-to-all-start.6 = ((bf16[8,5,16,768]{3,2,1,0:T(8,128)(2,1)}), bf16[8,5,16,768]{3,2,1,0:T(8,128)(2,1)S(1)}, u32[]{:S(2)}, u32[]{:S(2)}) async-start(bf16[8,5,16,768]{3,2,1,0:T(8,128)(2,1)} %get-tuple-element.159), calls=%async_computation.6 | async-start | bytes 1966080 | tf_op jit(solution)/shard_map/all_to_all | solution.py:923
  249.7 24.3 %dense_group.5 = (bf16[1,12,160,768]{3,2,1,0:T(8,128)(2,1)}, bf16[1,12,160,768]{3,2,1,0:T(8,128)(2,1)}, bf16[1920,768]{1,0:T(8,128)(2,1)}, bf16[1920,768]{1,0:T(...) custom-call(bf16[1,12,160,768]{3,2,1,0:T(8,128)(2,1)} %tokens_ref.9,, ...), custom_call_target="tpu_custom_call", output_to_operand_aliasing={{0}: (10, {}), {1}: (11, {}), {2}: (12, {}), {3}: (13, {}),... | custom-call | flops 28750000128 | bytes 31457280 | tf_op jit(solution)/shard_map/dense_group/pallas_call | solution.py:803
  274.0 6.2 %all-to-all-start.7 = ((bf16[8,5,16,768]{3,2,1,0:T(8,128)(2,1)}), bf16[8,5,16,768]{3,2,1,0:T(8,128)(2,1)S(1)}, u32[]{:S(2)}, u32[]{:S(2)}) async-start(bf16[8,5,16,768]{3,2,1,0:T(8,128)(2,1)} %get-tuple-element.161), calls=%async_computation.7 | async-start | bytes 1966080 | tf_op jit(solution)/shard_map/all_to_all | solution.py:923
  280.2 14.9 %in_weight_grad.1 = (bf16[384,3072]{1,0:T(8,128)(2,1)}, bf16[384,3072]{1,0:T(8,128)(2,1)}) custom-call(s32[1]{0:T(128)} %bitcast.41.pick_ref, bf16[1920,768]{1,0:T(8,128)(2,1)} %get-tuple-element.173.second_ref, bf16[1920,3072]{1,0:T(8,128)(2,1)} %get-tuple-element.174.grad_pre_ref), custom_call_target="tpu_custom_call" | custom-call | flops 1048576 | bytes 1048576 | tf_op jit(solution)/shard_map/in_weight_grad/pallas_call | solution.py:1011
  295.2 15.4 %out_weight_grad.1 = (bf16[2,2,384,768]{3,2,1,0:T(8,128)(2,1)}, bf16[2,2,384,768]{3,2,1,0:T(8,128)(2,1)}) custom-call(s32[1]{0:T(128)} %bitcast.41.pick_ref, bf16[1920,3072]{1,0:T(8,128)(2,1)} %get-tuple-element.169.act_ref, bf16[1920,768]{1,0:T(8,128)(2,1)} %get-tuple-element.170.grad_low_ref), custom_call_target="tpu_custom_call" | custom-call | flops 1048576 | bytes 1048576 | tf_op jit(solution)/shard_map/out_weight_grad/pallas_call | solution.py:1065
  311.9 18.5 %filter_backward.2 = (bf16[8,3,5,16,384]{4,3,2,1,0:T(8,128)(2,1)}, f32[384,768]{1,0:T(8,128)}, f32[768,384]{1,0:T(8,128)}, f32[8,384]{1,0:T(8,128)}) custom-call(s32[5]{0:T(128)} %and_select_fusion.pick_ref, bf16[8,5,16,768]{3,2,1,0:T(8,128)(2,1)} %copy-done.19, bf16[8,5,16,768]{3,2,1,0:T(8,128)(2,1)} %copy-done.20, bf16[8,5,16,768]{3,2,1,0:T(8,128)(2,1)} %copy-done.21, ...), custom_call_target="tpu_custom_call" | custom-call | flops 20700000256 | bytes 12582912 | tf_op jit(solution)/shard_map/filter_backward/pallas_call | solution.py:656
  330.5 6.0 %all-to-all-start.8 = ((bf16[8,3,5,16,384]{4,3,2,1,0:T(8,128)(2,1)}), bf16[8,3,5,16,384]{4,3,2,1,0:T(8,128)(2,1)}, u32[]{:S(2)}, u32[]{:S(2)}) async-start(bf16[8,3,5,16,384]{4,3,2,1,0:T(8,128)(2,1)} %get-tuple-element.166), calls=%async_computation.8 | async-start | bytes 2949120 | tf_op jit(solution)/shard_map/all_to_all | solution.py:923
  347.6 18.7 %filter_backward.3 = (bf16[8,3,5,16,384]{4,3,2,1,0:T(8,128)(2,1)}, f32[384,768]{1,0:T(8,128)}, f32[768,384]{1,0:T(8,128)}, f32[8,384]{1,0:T(8,128)}) custom-call(s32[5]{0:T(128)} %and_select_fusion.pick_ref, bf16[8,5,16,768]{3,2,1,0:T(8,128)(2,1)} %copy-done.19, bf16[8,5,16,768]{3,2,1,0:T(8,128)(2,1)} %copy-done.20, bf16[8,5,16,768]{3,2,1,0:T(8,128)(2,1)} %copy-done.21, ...), custom_call_target="tpu_custom_call" | custom-call | flops 20700000256 | bytes 12582912 | tf_op jit(solution)/shard_map/filter_backward/pallas_call | solution.py:656
  371.5 9.5 %collective-permute-done.14.got_one.got_two = bf16[768,768]{1,0:T(8,128)(2,1)S(1)} collective-permute-done((bf16[768,768]{1,0:T(8,128)(2,1)}, bf16[768,768]{1,0:T(8,128)(2,1)S(1)}, u32[]{:S(2)}, u32[]{:S(2)}) %collective-permute-start.14) | collective-permute-done | bytes 1179680 | tf_op jit(solution)/shard_map/ppermute | solution.py:932
  384.6 7.3 %all-to-all-start.9 = ((bf16[8,3,5,16,384]{4,3,2,1,0:T(8,128)(2,1)}), bf16[8,3,5,16,384]{4,3,2,1,0:T(8,128)(2,1)S(1)}, u32[]{:S(2)}, u32[]{:S(2)}) async-start(bf16[8,3,5,16,384]{4,3,2,1,0:T(8,128)(2,1)} %get-tuple-element.196), calls=%async_computation.9 | async-start | bytes 2949120 | tf_op jit(solution)/shard_map/all_to_all | solution.py:923
  405.7 6.4 %collective-permute-done.17 = f32[2,2,2,25,384]{4,2,3,1,0:T(2,128)} collective-permute-done((f32[2,2,2,25,384]{4,2,3,1,0:T(2,128)}, f32[2,2,2,25,384]{4,2,3,1,0:T(2,128)}, u32[]{:S(2)}, u32[]{:S(2)}) %collective-permute-start.17) | collective-permute-done | bytes 307232 | tf_op jit(solution)/shard_map/ppermute | solution.py:932
  415.7 9.1 %collective-permute-done.23.got_one.got_two = bf16[96,3072]{1,0:T(8,128)(2,1)S(1)} collective-permute-done((bf16[96,3072]{1,0:T(8,128)(2,1)}, bf16[96,3072]{1,0:T(8,128)(2,1)S(1)}, u32[]{:S(2)}, u32[]{:S(2)}) %collective-permute-start.23) | collective-permute-done | bytes 589856 | tf_op jit(solution)/shard_map/ppermute | solution.py:932
  427.7 3.8 collective-permute-start.24
  446.4 3.6 collective-permute-start.26
  453.3 9.8 %longitude_and_norm_grad.1 = f32[1,12,160,768]{3,2,1,0:T(8,128)} custom-call(bf16[1,12,160,768]{3,2,1,0:T(8,128)(2,1)} %tokens_ref.9, bf16[1,12,160,768]{3,2,1,0:T(8,128)(2,1)} %get-tuple-element.155.mixed_grad_ref, bf16[8,3,5,16,384]{4,3,2,1,0:T(8,128)(2,1)} %all-to-all-done.8.low_ref, bf16[8,3,5,16,384]{4,3,2,1,0:T(8,128)(2,1)} %copy-done.15, ...), custom_call_target="tpu_custom_call" | custom-call | flops 13799999488 | bytes 16777216 | tf_op jit(solution)/shard_map/longitude_and_norm_grad/pallas_call | solution.py:876
  (246 shorter events, 117.7 us)
Async XLA Ops:
  1.6 15.1 %collective-permute-start.1 = (bf16[96,768]{1,0:T(8,128)(2,1)S(1)}, bf16[96,768]{1,0:T(8,128)(2,1)S(1)}, u32[]{:S(2)}, u32[]{:S(2)}) collective-permute-start(bf16[96,768]{1,0:T(8,128)(2,1)S(1)} %convert_element_type.49), channel_id=1, source_target_pairs={{0,4},{1,5},{2,6},{3,7},{4,0},{5,1},{6,2},{7,3},{8,12},{9,13},{10,... | collective-permute-start | bytes 442376 | tf_op jit(solution)/shard_map/ppermute | solution.py:932
  6.7 12.3 %collective-permute-start = (bf16[24,3072]{1,0:T(8,128)(2,1)S(1)}, bf16[24,3072]{1,0:T(8,128)(2,1)S(1)}, u32[]{:S(2)}, u32[]{:S(2)}) collective-permute-start(bf16[24,3072]{1,0:T(8,128)(2,1)S(1)} %convert_element_type.48), channel_id=1, source_target_pairs={{0,4},{1,5},{2,6},{3,7},{4,0},{5,1},{6,2},{7,3},{8,12},{9,13},{10,... | collective-permute-start | bytes 442376 | tf_op jit(solution)/shard_map/ppermute | solution.py:932
  19.1 45.2 %all-to-all-start = ((bf16[8,17,16,384]{3,2,1,0:T(8,128)(2,1)}), bf16[8,17,16,384]{3,2,1,0:T(8,128)(2,1)S(1)}, u32[]{:S(2)}, u32[]{:S(2)}) async-start(bf16[8,17,16,384]{3,2,1,0:T(8,128)(2,1)} %get-tuple-element.125), calls=%async_computation | async-start | bytes 3342336 | tf_op jit(solution)/shard_map/all_to_all | solution.py:923
  24.9 35.6 %collective-permute-start.4 = (bf16[2,24,3072]{2,1,0:T(8,128)(2,1)S(1)}, bf16[2,24,3072]{2,1,0:T(8,128)(2,1)S(1)}, u32[]{:S(2)}, u32[]{:S(2)}) collective-permute-start(bf16[2,24,3072]{2,1,0:T(8,128)(2,1)S(1)} %pad_maximum_fusion.10), channel_id=1, source_target_pairs={{0,2},{1,3},{2,0},{3,1},{4,6},{5,7},{6,4},{7,5},{8,10},{9,11},{10,... | collective-permute-start | bytes 884744 | tf_op jit(solution)/shard_map/ppermute | solution.py:932
  28.2 38.8 %collective-permute-start.5 = (bf16[2,96,768]{2,1,0:T(8,128)(2,1)S(1)}, bf16[2,96,768]{2,1,0:T(8,128)(2,1)}, u32[]{:S(2)}, u32[]{:S(2)}) collective-permute-start(bf16[2,96,768]{2,1,0:T(8,128)(2,1)S(1)} %pad_maximum_fusion.11), channel_id=1, source_target_pairs={{0,2},{1,3},{2,0},{3,1},{4,6},{5,7},{6,4},{7,5},{8,10},{9,11},{10,... | collective-permute-start | bytes 884744 | tf_op jit(solution)/shard_map/ppermute | solution.py:932
  68.2 11.0 %collective-permute-start.3 = (bf16[2,8,32,384]{3,2,1,0:T(8,128)(2,1)S(1)}, bf16[2,8,32,384]{3,2,1,0:T(8,128)(2,1)S(1)}, u32[]{:S(2)}, u32[]{:S(2)}) collective-permute-start(bf16[2,8,32,384]{3,2,1,0:T(8,128)(2,1)S(1)} %pad_maximum_fusion.9), channel_id=1, source_target_pairs={{0,16},{16,0},{1,17},{17,1},{2,18},{18,2},{3,19},{19,3},{4,20},{20... | collective-permute-start | bytes 1179656 | tf_op jit(solution)/shard_map/ppermute | solution.py:932
  71.6 30.3 %collective-permute-start.9 = (bf16[2,2,96,768]{3,2,0,1:T(8,128)(2,1)}, bf16[2,2,96,768]{3,2,0,1:T(8,128)(2,1)}, u32[]{:S(2)}, u32[]{:S(2)}) collective-permute-start(bf16[2,2,96,768]{3,2,0,1:T(8,128)(2,1)} %pad_maximum_fusion.8), channel_id=1, source_target_pairs={{0,1},{1,0},{2,3},{3,2},{4,5},{5,4},{6,7},{7,6},{8,9},{9,8},{10,11... | collective-permute-start | bytes 1769480 | tf_op jit(solution)/shard_map/ppermute | solution.py:932
  73.0 41.2 %all-to-all-start.1 = ((bf16[8,15,16,384]{3,2,1,0:T(8,128)(2,1)}), bf16[8,15,16,384]{3,2,1,0:T(8,128)(2,1)}, u32[]{:S(2)}, u32[]{:S(2)}) async-start(bf16[8,15,16,384]{3,2,1,0:T(8,128)(2,1)} %get-tuple-element.129), calls=%async_computation.1 | async-start | bytes 2949120 | tf_op jit(solution)/shard_map/all_to_all | solution.py:923
  77.3 36.9 %collective-permute-start.6 = (bf16[2,2,24,3072]{3,2,0,1:T(8,128)(2,1)}, bf16[2,2,24,3072]{3,2,0,1:T(8,128)(2,1)}, u32[]{:S(2)}, u32[]{:S(2)}) collective-permute-start(bf16[2,2,24,3072]{3,2,0,1:T(8,128)(2,1)} %pad_maximum_fusion.7), channel_id=1, source_target_pairs={{0,1},{1,0},{2,3},{3,2},{4,5},{5,4},{6,7},{7,6},{8,9},{9,8},{10,11... | collective-permute-start | bytes 1769480 | tf_op jit(solution)/shard_map/ppermute | solution.py:932
  104.4 53.1 %collective-permute-start.10 = (bf16[2,2,2,96,768]{4,3,0,1,2:T(8,128)(2,1)}, bf16[2,2,2,96,768]{4,3,0,1,2:T(8,128)(2,1)}, u32[]{:S(2)}, u32[]{:S(2)}) collective-permute-start(bf16[2,2,2,96,768]{4,3,0,1,2:T(8,128)(2,1)} %pad_maximum_fusion.5), channel_id=1, source_target_pairs={{0,16},{16,0},{1,17},{17,1},{2,18},{18,2},{3,19},{19,3},{4,20},{20... | collective-permute-start | bytes 3538952 | tf_op jit(solution)/shard_map/ppermute | solution.py:932
  114.2 38.6 %all-to-all-start.2 = ((bf16[8,3,5,16,384]{4,3,2,1,0:T(8,128)(2,1)}), bf16[8,3,5,16,384]{4,3,2,1,0:T(8,128)(2,1)S(1)}, u32[]{:S(2)}, u32[]{:S(2)}) async-start(bf16[8,3,5,16,384]{4,3,2,1,0:T(8,128)(2,1)} %get-tuple-element.130), calls=%async_computation.2 | async-start | bytes 2949120 | tf_op jit(solution)/shard_map/all_to_all | solution.py:923
  121.6 39.1 %collective-permute-start.7 = (bf16[2,2,2,24,3072]{4,3,0,1,2:T(8,128)(2,1)}, bf16[2,2,2,24,3072]{4,3,0,1,2:T(8,128)(2,1)}, u32[]{:S(2)}, u32[]{:S(2)}) collective-permute-start(bf16[2,2,2,24,3072]{4,3,0,1,2:T(8,128)(2,1)} %pad_maximum_fusion.4), channel_id=1, source_target_pairs={{0,16},{16,0},{1,17},{17,1},{2,18},{18,2},{3,19},{19,3},{4,20},{20... | collective-permute-start | bytes 3538952 | tf_op jit(solution)/shard_map/ppermute | solution.py:932
  152.9 17.9 %all-to-all-start.3 = ((bf16[8,1,5,16,384]{4,3,2,1,0:T(8,128)(2,1)}), bf16[8,1,5,16,384]{4,3,2,1,0:T(8,128)(2,1)}, u32[]{:S(2)}, u32[]{:S(2)}) async-start(bf16[8,1,5,16,384]{4,3,2,1,0:T(8,128)(2,1)} %get-tuple-element.133), calls=%async_computation.3 | async-start | bytes 983040 | tf_op jit(solution)/shard_map/all_to_all | solution.py:923
  160.7 13.4 %collective-permute-start.11 = (bf16[2,2,2,2,96,768]{5,4,1,2,3,0:T(8,128)(2,1)}, bf16[2,2,2,2,96,768]{5,4,1,2,3,0:T(8,128)(2,1)}, u32[]{:S(2)}, u32[]{:S(2)}) collective-permute-start(bf16[2,2,2,2,96,768]{5,4,1,2,3,0:T(8,128)(2,1)} %pad_maximum_fusion.3), channel_id=1, source_target_pairs={{0,8},{8,0},{1,9},{9,1},{2,10},{10,2},{3,11},{11,3},{4,12},{12,4},... | collective-permute-start | bytes 7077896 | tf_op jit(solution)/shard_map/ppermute | solution.py:932
  179.2 32.9 %all-to-all-start.4 = ((bf16[8,2,5,16,384]{4,3,2,1,0:T(8,128)(2,1)}), bf16[8,2,5,16,384]{4,3,2,1,0:T(8,128)(2,1)S(1)}, u32[]{:S(2)}, u32[]{:S(2)}) async-start(bf16[8,2,5,16,384]{4,3,2,1,0:T(8,128)(2,1)} %get-tuple-element.134), calls=%async_computation.4 | async-start | bytes 1966080 | tf_op jit(solution)/shard_map/all_to_all | solution.py:923
  213.1 30.7 %all-to-all-start.5 = ((bf16[8,5,16,768]{3,2,1,0:T(8,128)(2,1)}), bf16[8,5,16,768]{3,2,1,0:T(8,128)(2,1)S(1)}, u32[]{:S(2)}, u32[]{:S(2)}) async-start(bf16[8,5,16,768]{3,2,1,0:T(8,128)(2,1)} %get-tuple-element.157), calls=%async_computation.5 | async-start | bytes 1966080 | tf_op jit(solution)/shard_map/all_to_all | solution.py:923
  243.9 30.1 %all-to-all-start.6 = ((bf16[8,5,16,768]{3,2,1,0:T(8,128)(2,1)}), bf16[8,5,16,768]{3,2,1,0:T(8,128)(2,1)S(1)}, u32[]{:S(2)}, u32[]{:S(2)}) async-start(bf16[8,5,16,768]{3,2,1,0:T(8,128)(2,1)} %get-tuple-element.159), calls=%async_computation.6 | async-start | bytes 1966080 | tf_op jit(solution)/shard_map/all_to_all | solution.py:923
  274.0 36.6 %all-to-all-start.7 = ((bf16[8,5,16,768]{3,2,1,0:T(8,128)(2,1)}), bf16[8,5,16,768]{3,2,1,0:T(8,128)(2,1)S(1)}, u32[]{:S(2)}, u32[]{:S(2)}) async-start(bf16[8,5,16,768]{3,2,1,0:T(8,128)(2,1)} %get-tuple-element.161), calls=%async_computation.7 | async-start | bytes 1966080 | tf_op jit(solution)/shard_map/all_to_all | solution.py:923
  310.6 25.9 %collective-permute-start.12 = (bf16[384,3072]{1,0:T(8,128)(2,1)}, bf16[384,3072]{1,0:T(8,128)(2,1)}, u32[]{:S(2)}, u32[]{:S(2)}) collective-permute-start(bf16[384,3072]{1,0:T(8,128)(2,1)} %get-tuple-element.178), channel_id=1, source_target_pairs={{0,8},{8,0},{1,9},{9,1},{2,10},{10,2},{3,11},{11,3},{4,12},{12,4},... | collective-permute-start | bytes 7077896 | tf_op jit(solution)/shard_map/ppermute | solution.py:932
  310.7 29.9 %collective-permute-start.13 = (bf16[1536,768]{1,0:T(8,128)(2,1)}, bf16[1536,768]{1,0:T(8,128)(2,1)S(1)}, u32[]{:S(2)}, u32[]{:S(2)}) collective-permute-start(bf16[1536,768]{1,0:T(8,128)(2,1)} %bitcast.133), channel_id=1, source_target_pairs={{0,8},{8,0},{1,9},{9,1},{2,10},{10,2},{3,11},{11,3},{4,12},{12,4},... | collective-permute-start | bytes 7077896 | tf_op jit(solution)/shard_map/ppermute | solution.py:932
  330.5 54.1 %all-to-all-start.8 = ((bf16[8,3,5,16,384]{4,3,2,1,0:T(8,128)(2,1)}), bf16[8,3,5,16,384]{4,3,2,1,0:T(8,128)(2,1)}, u32[]{:S(2)}, u32[]{:S(2)}) async-start(bf16[8,3,5,16,384]{4,3,2,1,0:T(8,128)(2,1)} %get-tuple-element.166), calls=%async_computation.8 | async-start | bytes 2949120 | tf_op jit(solution)/shard_map/all_to_all | solution.py:923
  340.1 27.9 %collective-permute-start.15 = (bf16[192,3072]{1,0:T(8,128)(2,1)}, bf16[192,3072]{1,0:T(8,128)(2,1)S(1)}, u32[]{:S(2)}, u32[]{:S(2)}) collective-permute-start(bf16[192,3072]{1,0:T(8,128)(2,1)} %get-tuple-element.180), channel_id=1, source_target_pairs={{0,16},{16,0},{1,17},{17,1},{2,18},{18,2},{3,19},{19,3},{4,20},{20... | collective-permute-start | bytes 3538952 | tf_op jit(solution)/shard_map/ppermute | solution.py:932
  345.5 35.5 %collective-permute-start.14 = (bf16[768,768]{1,0:T(8,128)(2,1)}, bf16[768,768]{1,0:T(8,128)(2,1)S(1)}, u32[]{:S(2)}, u32[]{:S(2)}) collective-permute-start(bf16[768,768]{1,0:T(8,128)(2,1)} %get-tuple-element.184), channel_id=1, source_target_pairs={{0,1},{1,0},{2,3},{3,2},{4,5},{5,4},{6,7},{7,6},{8,9},{9,8},{10,11... | collective-permute-start | bytes 3538952 | tf_op jit(solution)/shard_map/ppermute | solution.py:932
  384.6 49.9 %all-to-all-start.9 = ((bf16[8,3,5,16,384]{4,3,2,1,0:T(8,128)(2,1)}), bf16[8,3,5,16,384]{4,3,2,1,0:T(8,128)(2,1)S(1)}, u32[]{:S(2)}, u32[]{:S(2)}) async-start(bf16[8,3,5,16,384]{4,3,2,1,0:T(8,128)(2,1)} %get-tuple-element.196), calls=%async_computation.9 | async-start | bytes 2949120 | tf_op jit(solution)/shard_map/all_to_all | solution.py:923
  402.2 22.6 %collective-permute-start.23 = (bf16[96,3072]{1,0:T(8,128)(2,1)}, bf16[96,3072]{1,0:T(8,128)(2,1)S(1)}, u32[]{:S(2)}, u32[]{:S(2)}) collective-permute-start(bf16[96,3072]{1,0:T(8,128)(2,1)} %get-tuple-element.195), channel_id=1, source_target_pairs={{0,1},{1,0},{2,3},{3,2},{4,5},{5,4},{6,7},{7,6},{8,9},{9,8},{10,11... | collective-permute-start | bytes 1769480 | tf_op jit(solution)/shard_map/ppermute | solution.py:932
  404.3 27.2 %collective-permute-start.21 = (bf16[384,768]{1,0:T(8,128)(2,1)}, bf16[384,768]{1,0:T(8,128)(2,1)S(1)}, u32[]{:S(2)}, u32[]{:S(2)}) collective-permute-start(bf16[384,768]{1,0:T(8,128)(2,1)} %get-tuple-element.193), channel_id=1, source_target_pairs={{0,16},{16,0},{1,17},{17,1},{2,18},{18,2},{3,19},{19,3},{4,20},{20... | collective-permute-start | bytes 1769480 | tf_op jit(solution)/shard_map/ppermute | solution.py:932
  413.6 20.8 %collective-permute-start.18 = (f32[2,2,25,384]{3,1,2,0:T(2,128)S(1)}, f32[2,2,25,384]{3,1,2,0:T(2,128)S(1)}, u32[]{:S(2)}, u32[]{:S(2)}) collective-permute-start(f32[2,2,25,384]{3,1,2,0:T(2,128)S(1)} %bitcast.127), channel_id=1, source_target_pairs={{0,1},{1,0},{2,3},{3,2},{4,5},{5,4},{6,7},{7,6},{8,9},{9,8},{10,11... | collective-permute-start | bytes 460808 | tf_op jit(solution)/shard_map/ppermute | solution.py:932
  427.7 11.5 %collective-permute-start.24 = (bf16[48,3072]{1,0:T(8,128)(2,1)}, bf16[48,3072]{1,0:T(8,128)(2,1)S(1)}, u32[]{:S(2)}, u32[]{:S(2)}) collective-permute-start(bf16[48,3072]{1,0:T(8,128)(2,1)} %get-tuple-element.219), channel_id=1, source_target_pairs={{0,2},{1,3},{2,0},{3,1},{4,6},{5,7},{6,4},{7,5},{8,10},{9,11},{10,... | collective-permute-start | bytes 884744 | tf_op jit(solution)/shard_map/ppermute | solution.py:932
  434.7 15.4 %collective-permute-start.19 = (f32[2,25,384]{2,0,1:T(2,128)S(1)}, f32[2,25,384]{2,0,1:T(2,128)S(1)}, u32[]{:S(2)}, u32[]{:S(2)}) collective-permute-start(f32[2,25,384]{2,0,1:T(2,128)S(1)} %bitcast.128), channel_id=1, source_target_pairs={{0,2},{1,3},{2,0},{3,1},{4,6},{5,7},{6,4},{7,5},{8,10},{9,11},{10,... | collective-permute-start | bytes 230408 | tf_op jit(solution)/shard_map/ppermute | solution.py:932
  446.4 18.7 %collective-permute-start.26 = (bf16[96,768]{1,0:T(8,128)(2,1)}, bf16[96,768]{1,0:T(8,128)(2,1)S(1)}, u32[]{:S(2)}, u32[]{:S(2)}) collective-permute-start(bf16[96,768]{1,0:T(8,128)(2,1)} %get-tuple-element.225), channel_id=1, source_target_pairs={{0,4},{1,5},{2,6},{3,7},{4,0},{5,1},{6,2},{7,3},{8,12},{9,13},{10,... | collective-permute-start | bytes 442376 | tf_op jit(solution)/shard_map/ppermute | solution.py:932
  450.0 16.3 %collective-permute-start.25 = (bf16[24,3072]{1,0:T(8,128)(2,1)S(1)}, bf16[24,3072]{1,0:T(8,128)(2,1)S(1)}, u32[]{:S(2)}, u32[]{:S(2)}) collective-permute-start(bf16[24,3072]{1,0:T(8,128)(2,1)S(1)} %copy-done.51), channel_id=1, source_target_pairs={{0,4},{1,5},{2,6},{3,7},{4,0},{5,1},{6,2},{7,3},{8,12},{9,13},{10,... | collective-permute-start | bytes 442376 | tf_op jit(solution)/shard_map/ppermute | solution.py:932
  450.3 13.4 %collective-permute-start.20 = (f32[25,384]{1,0:T(8,128)S(1)}, f32[25,384]{1,0:T(8,128)S(1)}, u32[]{:S(2)}, u32[]{:S(2)}) collective-permute-start(f32[25,384]{1,0:T(8,128)S(1)} %bitcast.129), channel_id=1, source_target_pairs={{0,4},{1,5},{2,6},{3,7},{4,0},{5,1},{6,2},{7,3},{8,12},{9,13},{10,... | collective-permute-start | bytes 115208 | tf_op jit(solution)/shard_map/ppermute | solution.py:932
  (57 other events, 424.1 us)
where the time goes:
time: 478 us; the launch traced here: 469 us
  Pallas kernels  205 us (43%)
  waiting for transfers between devices  112 us (23%)
  starting transfers between devices  88.5 us (19%)
  other arithmetic  30.9 us (6%)
  local copies, waits for them, and re-layouts  27 us (6%)
    ppermute x27, waiting for transfers between devices, swap(): lax.ppermute(values, axis, [(i, i ^ bit) for i in range(SIZES[axis])])  80.9 us
    pallas_call x3, Pallas kernels, dense(): pl.pallas_call(dense_body, name='dense_group', grid=(hidden // FCHUNK,),...  72.8 us
    all_to_all x10, starting transfers between devices, exchange(): return lax.all_to_all(values, 'sp', split_axis=0, concat_axis=0, tiled=True)  54.5 us
    pallas_call x2, Pallas kernels, filter_backward(): pl.pallas_call(functools.partial(filter_back_body, groups), name='filter_...  37.2 us
    ppermute x27, starting transfers between devices, swap(): lax.ppermute(values, axis, [(i, i ^ bit) for i in range(SIZES[axis])])  34 us
    all_to_all x10, waiting for transfers between devices, exchange(): return lax.all_to_all(values, 'sp', split_axis=0, concat_axis=0, tiled=True)  30.9 us
    pallas_call x2, Pallas kernels, filter_forward(): pl.pallas_call(functools.partial(filter_body, pieces), name='filter_forwa...  27.7 us
    pallas_call x8, Pallas kernels, add_split(): pl.pallas_call(add_split_body, name='add_split', grid_spec=pltpu.Prefetch...  20 us
  transfers between devices with their start and end apart: 37, of which 17 were waited for; matrix products, arithmetic and copies ran while one was open for 10% of the time, Pallas kernels for 44%

commit v1 on v0

--- a/solution.py
+++ b/solution.py
@@ -607,8 +607,9 @@
     both = jnp.concatenate([modes_re.astype(BF16), modes_im.astype(BF16)], axis=0)
     sent = dot(inverse_ref[0], both, 1, 0).astype(BF16)
     sent_ref[...] = sent.reshape(sent_ref.shape)
-    one_part = dot(modes_ref[0, :ROWS], out_re, 0, 0) + dot(modes_ref[0, ROWS:], out_im, 0, 0)
-    two_part = dot(sums_ref[0, 0], grad_re, 0, 0) + dot(sums_ref[0, 1], grad_im, 0, 0)
+    one_part = dot(modes_ref[0], jnp.concatenate([out_re, out_im], axis=0), 0, 0)
+    sums = sums_ref[...].reshape(2 * ROWS, 2 * HALF)
+    two_part = dot(sums, grad.astype(BF16), 0, 0)
     gain_part = sent.astype(F32) * stacked(normed_refs).astype(F32)
     shift_part = modes_re * shift_row_ref[0, :, 0:1]
     rows = [

time: 478 us -> 478 us (level)
  no operation moved by 1% of the time
where the time goes in v1:
time: 478 us; the launch traced here: 468 us
  Pallas kernels  205 us (43%)
  waiting for transfers between devices  112 us (23%)
  starting transfers between devices  88.5 us (19%)
  other arithmetic  30.9 us (6%)
  local copies, waits for them, and re-layouts  27 us (6%)
    ppermute x27, waiting for transfers between devices, swap(): lax.ppermute(values, axis, [(i, i ^ bit) for i in range(SIZES[axis])])  81 us
    pallas_call x3, Pallas kernels, dense(): pl.pallas_call(dense_body, name='dense_group', grid=(hidden // FCHUNK,),...  72.8 us
    all_to_all x10, starting transfers between devices, exchange(): return lax.all_to_all(values, 'sp', split_axis=0, concat_axis=0, tiled=True)  54.5 us
    pallas_call x2, Pallas kernels, filter_backward(): pl.pallas_call(functools.partial(filter_back_body, groups), name='filter_...  37.1 us
    ppermute x27, starting transfers between devices, swap(): lax.ppermute(values, axis, [(i, i ^ bit) for i in range(SIZES[axis])])  34 us
    all_to_all x10, waiting for transfers between devices, exchange(): return lax.all_to_all(values, 'sp', split_axis=0, concat_axis=0, tiled=True)  30.9 us
    pallas_call x2, Pallas kernels, filter_forward(): pl.pallas_call(functools.partial(filter_body, pieces), name='filter_forwa...  27.7 us
    pallas_call x8, Pallas kernels, add_split(): pl.pallas_call(add_split_body, name='add_split', grid_spec=pltpu.Prefetch...  20 us
  transfers between devices with their start and end apart: 37, of which 17 were waited for; matrix products, arithmetic and copies ran while one was open for 10% of the time, Pallas kernels for 44%

profile of v1, /device:TPU:0, one launch (start us, length us, event | category | flops | bytes accessed | tf_op | source)
XLA Modules:
  0.0 468.5 jit_solution(16025212334664545845)
XLA Ops:
  1.6 4.1 collective-permute-start.1
  8.1 7.1 %norm_and_longitude.1 = (bf16[8,17,16,384]{3,2,1,0:T(8,128)(2,1)}, bf16[8,15,16,384]{3,2,1,0:T(8,128)(2,1)}) custom-call(bf16[1,12,160,768]{3,2,1,0:T(8,128)(2,1)} %tokens_ref.9, bf16[640,640]{1,0:T(8,128)(2,1)} %constant.317.clone.table_ref, f32[24,384]{1,0:T(8,128)} %filter_ref.1, f32[1,384]{1,0:T(1,128)} %reshape.123.small_ref), custom_call_target="tpu_custom_call" | custom-call | flops 8049999872 | bytes 2949120 | tf_op jit(solution)/shard_map/norm_and_longitude/pallas_call | solution.py:435
  19.1 5.8 %all-to-all-start = ((bf16[8,17,16,384]{3,2,1,0:T(8,128)(2,1)}), bf16[8,17,16,384]{3,2,1,0:T(8,128)(2,1)S(1)}, u32[]{:S(2)}, u32[]{:S(2)}) async-start(bf16[8,17,16,384]{3,2,1,0:T(8,128)(2,1)} %get-tuple-element.125), calls=%async_computation | async-start | bytes 3342336 | tf_op jit(solution)/shard_map/all_to_all | solution.py:924
  28.3 32.2 %collective-permute-done.4 = bf16[2,24,3072]{2,1,0:T(8,128)(2,1)S(1)} collective-permute-done((bf16[2,24,3072]{2,1,0:T(8,128)(2,1)S(1)}, bf16[2,24,3072]{2,1,0:T(8,128)(2,1)S(1)}, u32[]{:S(2)}, u32[]{:S(2)}) %collective-permute-start.4) | collective-permute-done | bytes 294944 | tf_op jit(solution)/shard_map/ppermute | solution.py:933
  60.5 3.8 all-to-all-done.refs_0_.refs_1_.refs_2_.refs_8_.refs_9_.refs_10_
  73.0 4.3 all-to-all-start.1
  88.1 13.8 %filter_forward.2 = (bf16[8,3,5,16,384]{4,3,2,1,0:T(8,128)(2,1)}, bf16[5,416,384]{2,1,0:T(8,128)(2,1)}, bf16[5,2,208,768]{3,2,1,0:T(8,128)(2,1)}, bf16[5,4,208,384]{3,2,1,0:T(8,128)(2,1)}) custom-call(s32[5]{0:T(128)} %and_select_fusion.pick_ref, bf16[8,17,16,384]{3,2,1,0:T(8,128)(2,1)} %copy-done.14, bf16[8,17,16,384]{3,2,1,0:T(8,128)(2,1)} %copy-done.14, ...), custom_call_target="tpu_custom_call" | custom-call | flops 16099999744 | bytes 12582912 | tf_op jit(solution)/shard_map/filter_forward/pallas_call | solution.py:544
  104.9 9.3 %collective-permute-done.6 = bf16[2,2,24,3072]{3,2,0,1:T(8,128)(2,1)} collective-permute-done((bf16[2,2,24,3072]{3,2,0,1:T(8,128)(2,1)}, bf16[2,2,24,3072]{3,2,0,1:T(8,128)(2,1)}, u32[]{:S(2)}, u32[]{:S(2)}) %collective-permute-start.6) | collective-permute-done | bytes 589856 | tf_op jit(solution)/shard_map/ppermute | solution.py:933
  114.2 4.6 all-to-all-start.2
  122.1 13.9 %filter_forward.3 = (bf16[8,1,5,16,384]{4,3,2,1,0:T(8,128)(2,1)}, bf16[8,2,5,16,384]{4,3,2,1,0:T(8,128)(2,1)}, bf16[5,416,384]{2,1,0:T(8,128)(2,1)}, bf16[5,2,20...) custom-call(s32[5]{0:T(128)} %and_select_fusion.pick_ref, ...), custom_call_target="tpu_custom_call" | custom-call | flops 16099999744 | bytes 12582912 | tf_op jit(solution)/shard_map/filter_forward/pallas_call | solution.py:544
  136.0 16.8 %all-to-all-done.2.low_ref = bf16[8,3,5,16,384]{4,3,2,1,0:T(8,128)(2,1)S(1)} async-done(((bf16[8,3,5,16,384]{4,3,2,1,0:T(8,128)(2,1)}), bf16[8,3,5,16,384]{4,3,2,1,0:T(8,128)(2,1)S(1)}, u32[]{:S(2)}, u32[]{:S(2)}) %all-to-all-start.2) | async-done | bytes 1474592 | tf_op jit(solution)/shard_map/all_to_all | solution.py:924
  152.9 4.6 all-to-all-start.3
  160.7 10.0 %all-to-all-done.3.high_ref = bf16[8,1,5,16,384]{4,3,2,1,0:T(8,128)(2,1)} async-done(((bf16[8,1,5,16,384]{4,3,2,1,0:T(8,128)(2,1)}), bf16[8,1,5,16,384]{4,3,2,1,0:T(8,128)(2,1)}, u32[]{:S(2)}, u32[]{:S(2)}) %all-to-all-start.3) | async-done | bytes 491552 | tf_op jit(solution)/shard_map/all_to_all | solution.py:924
  179.2 3.6 all-to-all-start.4
  187.9 24.2 %dense_group.3 = (bf16[1,12,160,768]{3,2,1,0:T(8,128)(2,1)}, bf16[1,12,160,768]{3,2,1,0:T(8,128)(2,1)}, bf16[1920,768]{1,0:T(8,128)(2,1)}, bf16[1920,768]{1,0:T(...) custom-call(bf16[1,12,160,768]{3,2,1,0:T(8,128)(2,1)} %tokens_ref.9,, ...), custom_call_target="tpu_custom_call" | custom-call | flops 28750000128 | bytes 31457280 | tf_op jit(solution)/shard_map/dense_group/pallas_call | solution.py:804
  213.1 6.2 %all-to-all-start.5 = ((bf16[8,5,16,768]{3,2,1,0:T(8,128)(2,1)}), bf16[8,5,16,768]{3,2,1,0:T(8,128)(2,1)S(1)}, u32[]{:S(2)}, u32[]{:S(2)}) async-start(bf16[8,5,16,768]{3,2,1,0:T(8,128)(2,1)} %get-tuple-element.157), calls=%async_computation.5 | async-start | bytes 1966080 | tf_op jit(solution)/shard_map/all_to_all | solution.py:924
  219.3 24.3 %dense_group.4 = (bf16[1,12,160,768]{3,2,1,0:T(8,128)(2,1)}, bf16[1,12,160,768]{3,2,1,0:T(8,128)(2,1)}, bf16[1920,768]{1,0:T(8,128)(2,1)}, bf16[1920,768]{1,0:T(...) custom-call(bf16[1,12,160,768]{3,2,1,0:T(8,128)(2,1)} %tokens_ref.9,, ...), custom_call_target="tpu_custom_call", output_to_operand_aliasing={{0}: (10, {}), {1}: (11, {}), {2}: (12, {}), {3}: (13, {}),... | custom-call | flops 28750000128 | bytes 31457280 | tf_op jit(solution)/shard_map/dense_group/pallas_call | solution.py:804
  243.9 5.8 %all-to-all-start.6 = ((bf16[8,5,16,768]{3,2,1,0:T(8,128)(2,1)}), bf16[8,5,16,768]{3,2,1,0:T(8,128)(2,1)S(1)}, u32[]{:S(2)}, u32[]{:S(2)}) async-start(bf16[8,5,16,768]{3,2,1,0:T(8,128)(2,1)} %get-tuple-element.159), calls=%async_computation.6 | async-start | bytes 1966080 | tf_op jit(solution)/shard_map/all_to_all | solution.py:924
  249.7 24.3 %dense_group.5 = (bf16[1,12,160,768]{3,2,1,0:T(8,128)(2,1)}, bf16[1,12,160,768]{3,2,1,0:T(8,128)(2,1)}, bf16[1920,768]{1,0:T(8,128)(2,1)}, bf16[1920,768]{1,0:T(...) custom-call(bf16[1,12,160,768]{3,2,1,0:T(8,128)(2,1)} %tokens_ref.9,, ...), custom_call_target="tpu_custom_call", output_to_operand_aliasing={{0}: (10, {}), {1}: (11, {}), {2}: (12, {}), {3}: (13, {}),... | custom-call | flops 28750000128 | bytes 31457280 | tf_op jit(solution)/shard_map/dense_group/pallas_call | solution.py:804
  274.0 6.2 %all-to-all-start.7 = ((bf16[8,5,16,768]{3,2,1,0:T(8,128)(2,1)}), bf16[8,5,16,768]{3,2,1,0:T(8,128)(2,1)S(1)}, u32[]{:S(2)}, u32[]{:S(2)}) async-start(bf16[8,5,16,768]{3,2,1,0:T(8,128)(2,1)} %get-tuple-element.161), calls=%async_computation.7 | async-start | bytes 1966080 | tf_op jit(solution)/shard_map/all_to_all | solution.py:924
  280.2 14.9 %in_weight_grad.1 = (bf16[384,3072]{1,0:T(8,128)(2,1)}, bf16[384,3072]{1,0:T(8,128)(2,1)}) custom-call(s32[1]{0:T(128)} %bitcast.41.pick_ref, bf16[1920,768]{1,0:T(8,128)(2,1)} %get-tuple-element.173.second_ref, bf16[1920,3072]{1,0:T(8,128)(2,1)} %get-tuple-element.174.grad_pre_ref), custom_call_target="tpu_custom_call" | custom-call | flops 1048576 | bytes 1048576 | tf_op jit(solution)/shard_map/in_weight_grad/pallas_call | solution.py:1012
  295.2 15.4 %out_weight_grad.1 = (bf16[2,2,384,768]{3,2,1,0:T(8,128)(2,1)}, bf16[2,2,384,768]{3,2,1,0:T(8,128)(2,1)}) custom-call(s32[1]{0:T(128)} %bitcast.41.pick_ref, bf16[1920,3072]{1,0:T(8,128)(2,1)} %get-tuple-element.169.act_ref, bf16[1920,768]{1,0:T(8,128)(2,1)} %get-tuple-element.170.grad_low_ref), custom_call_target="tpu_custom_call" | custom-call | flops 1048576 | bytes 1048576 | tf_op jit(solution)/shard_map/out_weight_grad/pallas_call | solution.py:1066
  311.9 18.5 %filter_backward.2 = (bf16[8,3,5,16,384]{4,3,2,1,0:T(8,128)(2,1)}, f32[384,768]{1,0:T(8,128)}, f32[768,384]{1,0:T(8,128)}, f32[8,384]{1,0:T(8,128)}) custom-call(s32[5]{0:T(128)} %and_select_fusion.pick_ref, bf16[8,5,16,768]{3,2,1,0:T(8,128)(2,1)} %copy-done.19, bf16[8,5,16,768]{3,2,1,0:T(8,128)(2,1)} %copy-done.20, bf16[8,5,16,768]{3,2,1,0:T(8,128)(2,1)} %copy-done.21, ...), custom_call_target="tpu_custom_call" | custom-call | flops 20700000256 | bytes 12582912 | tf_op jit(solution)/shard_map/filter_backward/pallas_call | solution.py:657
  330.4 6.0 %all-to-all-start.8 = ((bf16[8,3,5,16,384]{4,3,2,1,0:T(8,128)(2,1)}), bf16[8,3,5,16,384]{4,3,2,1,0:T(8,128)(2,1)}, u32[]{:S(2)}, u32[]{:S(2)}) async-start(bf16[8,3,5,16,384]{4,3,2,1,0:T(8,128)(2,1)} %get-tuple-element.166), calls=%async_computation.8 | async-start | bytes 2949120 | tf_op jit(solution)/shard_map/all_to_all | solution.py:924
  347.5 18.6 %filter_backward.3 = (bf16[8,3,5,16,384]{4,3,2,1,0:T(8,128)(2,1)}, f32[384,768]{1,0:T(8,128)}, f32[768,384]{1,0:T(8,128)}, f32[8,384]{1,0:T(8,128)}) custom-call(s32[5]{0:T(128)} %and_select_fusion.pick_ref, bf16[8,5,16,768]{3,2,1,0:T(8,128)(2,1)} %copy-done.19, bf16[8,5,16,768]{3,2,1,0:T(8,128)(2,1)} %copy-done.20, bf16[8,5,16,768]{3,2,1,0:T(8,128)(2,1)} %copy-done.21, ...), custom_call_target="tpu_custom_call" | custom-call | flops 20700000256 | bytes 12582912 | tf_op jit(solution)/shard_map/filter_backward/pallas_call | solution.py:657
  371.5 9.5 %collective-permute-done.14.got_one.got_two = bf16[768,768]{1,0:T(8,128)(2,1)S(1)} collective-permute-done((bf16[768,768]{1,0:T(8,128)(2,1)}, bf16[768,768]{1,0:T(8,128)(2,1)S(1)}, u32[]{:S(2)}, u32[]{:S(2)}) %collective-permute-start.14) | collective-permute-done | bytes 1179680 | tf_op jit(solution)/shard_map/ppermute | solution.py:933
  384.6 7.3 %all-to-all-start.9 = ((bf16[8,3,5,16,384]{4,3,2,1,0:T(8,128)(2,1)}), bf16[8,3,5,16,384]{4,3,2,1,0:T(8,128)(2,1)S(1)}, u32[]{:S(2)}, u32[]{:S(2)}) async-start(bf16[8,3,5,16,384]{4,3,2,1,0:T(8,128)(2,1)} %get-tuple-element.196), calls=%async_computation.9 | async-start | bytes 2949120 | tf_op jit(solution)/shard_map/all_to_all | solution.py:924
  405.7 6.4 %collective-permute-done.17 = f32[2,2,2,25,384]{4,2,3,1,0:T(2,128)} collective-permute-done((f32[2,2,2,25,384]{4,2,3,1,0:T(2,128)}, f32[2,2,2,25,384]{4,2,3,1,0:T(2,128)}, u32[]{:S(2)}, u32[]{:S(2)}) %collective-permute-start.17) | collective-permute-done | bytes 307232 | tf_op jit(solution)/shard_map/ppermute | solution.py:933
  415.6 9.1 %collective-permute-done.23.got_one.got_two = bf16[96,3072]{1,0:T(8,128)(2,1)S(1)} collective-permute-done((bf16[96,3072]{1,0:T(8,128)(2,1)}, bf16[96,3072]{1,0:T(8,128)(2,1)S(1)}, u32[]{:S(2)}, u32[]{:S(2)}) %collective-permute-start.23) | collective-permute-done | bytes 589856 | tf_op jit(solution)/shard_map/ppermute | solution.py:933
  427.7 3.8 collective-permute-start.24
  446.4 3.6 collective-permute-start.26
  453.3 9.8 %longitude_and_norm_grad.1 = f32[1,12,160,768]{3,2,1,0:T(8,128)} custom-call(bf16[1,12,160,768]{3,2,1,0:T(8,128)(2,1)} %tokens_ref.9, bf16[1,12,160,768]{3,2,1,0:T(8,128)(2,1)} %get-tuple-element.155.mixed_grad_ref, bf16[8,3,5,16,384]{4,3,2,1,0:T(8,128)(2,1)} %all-to-all-done.8.low_ref, bf16[8,3,5,16,384]{4,3,2,1,0:T(8,128)(2,1)} %copy-done.15, ...), custom_call_target="tpu_custom_call" | custom-call | flops 13799999488 | bytes 16777216 | tf_op jit(solution)/shard_map/longitude_and_norm_grad/pallas_call | solution.py:877
  (246 shorter events, 117.8 us)
Async XLA Ops:
  1.6 15.1 %collective-permute-start.1 = (bf16[96,768]{1,0:T(8,128)(2,1)S(1)}, bf16[96,768]{1,0:T(8,128)(2,1)S(1)}, u32[]{:S(2)}, u32[]{:S(2)}) collective-permute-start(bf16[96,768]{1,0:T(8,128)(2,1)S(1)} %convert_element_type.49), channel_id=1, source_target_pairs={{0,4},{1,5},{2,6},{3,7},{4,0},{5,1},{6,2},{7,3},{8,12},{9,13},{10,... | collective-permute-start | bytes 442376 | tf_op jit(solution)/shard_map/ppermute | solution.py:933
  6.7 12.3 %collective-permute-start = (bf16[24,3072]{1,0:T(8,128)(2,1)S(1)}, bf16[24,3072]{1,0:T(8,128)(2,1)S(1)}, u32[]{:S(2)}, u32[]{:S(2)}) collective-permute-start(bf16[24,3072]{1,0:T(8,128)(2,1)S(1)} %convert_element_type.48), channel_id=1, source_target_pairs={{0,4},{1,5},{2,6},{3,7},{4,0},{5,1},{6,2},{7,3},{8,12},{9,13},{10,... | collective-permute-start | bytes 442376 | tf_op jit(solution)/shard_map/ppermute | solution.py:933
  19.1 45.2 %all-to-all-start = ((bf16[8,17,16,384]{3,2,1,0:T(8,128)(2,1)}), bf16[8,17,16,384]{3,2,1,0:T(8,128)(2,1)S(1)}, u32[]{:S(2)}, u32[]{:S(2)}) async-start(bf16[8,17,16,384]{3,2,1,0:T(8,128)(2,1)} %get-tuple-element.125), calls=%async_computation | async-start | bytes 3342336 | tf_op jit(solution)/shard_map/all_to_all | solution.py:924
  24.9 35.6 %collective-permute-start.4 = (bf16[2,24,3072]{2,1,0:T(8,128)(2,1)S(1)}, bf16[2,24,3072]{2,1,0:T(8,128)(2,1)S(1)}, u32[]{:S(2)}, u32[]{:S(2)}) collective-permute-start(bf16[2,24,3072]{2,1,0:T(8,128)(2,1)S(1)} %pad_maximum_fusion.10), channel_id=1, source_target_pairs={{0,2},{1,3},{2,0},{3,1},{4,6},{5,7},{6,4},{7,5},{8,10},{9,11},{10,... | collective-permute-start | bytes 884744 | tf_op jit(solution)/shard_map/ppermute | solution.py:933
  28.2 38.8 %collective-permute-start.5 = (bf16[2,96,768]{2,1,0:T(8,128)(2,1)S(1)}, bf16[2,96,768]{2,1,0:T(8,128)(2,1)}, u32[]{:S(2)}, u32[]{:S(2)}) collective-permute-start(bf16[2,96,768]{2,1,0:T(8,128)(2,1)S(1)} %pad_maximum_fusion.11), channel_id=1, source_target_pairs={{0,2},{1,3},{2,0},{3,1},{4,6},{5,7},{6,4},{7,5},{8,10},{9,11},{10,... | collective-permute-start | bytes 884744 | tf_op jit(solution)/shard_map/ppermute | solution.py:933
  68.2 11.0 %collective-permute-start.3 = (bf16[2,8,32,384]{3,2,1,0:T(8,128)(2,1)S(1)}, bf16[2,8,32,384]{3,2,1,0:T(8,128)(2,1)S(1)}, u32[]{:S(2)}, u32[]{:S(2)}) collective-permute-start(bf16[2,8,32,384]{3,2,1,0:T(8,128)(2,1)S(1)} %pad_maximum_fusion.9), channel_id=1, source_target_pairs={{0,16},{16,0},{1,17},{17,1},{2,18},{18,2},{3,19},{19,3},{4,20},{20... | collective-permute-start | bytes 1179656 | tf_op jit(solution)/shard_map/ppermute | solution.py:933
  71.6 30.3 %collective-permute-start.9 = (bf16[2,2,96,768]{3,2,0,1:T(8,128)(2,1)}, bf16[2,2,96,768]{3,2,0,1:T(8,128)(2,1)}, u32[]{:S(2)}, u32[]{:S(2)}) collective-permute-start(bf16[2,2,96,768]{3,2,0,1:T(8,128)(2,1)} %pad_maximum_fusion.8), channel_id=1, source_target_pairs={{0,1},{1,0},{2,3},{3,2},{4,5},{5,4},{6,7},{7,6},{8,9},{9,8},{10,11... | collective-permute-start | bytes 1769480 | tf_op jit(solution)/shard_map/ppermute | solution.py:933
  73.0 41.2 %all-to-all-start.1 = ((bf16[8,15,16,384]{3,2,1,0:T(8,128)(2,1)}), bf16[8,15,16,384]{3,2,1,0:T(8,128)(2,1)}, u32[]{:S(2)}, u32[]{:S(2)}) async-start(bf16[8,15,16,384]{3,2,1,0:T(8,128)(2,1)} %get-tuple-element.129), calls=%async_computation.1 | async-start | bytes 2949120 | tf_op jit(solution)/shard_map/all_to_all | solution.py:924
  77.3 36.9 %collective-permute-start.6 = (bf16[2,2,24,3072]{3,2,0,1:T(8,128)(2,1)}, bf16[2,2,24,3072]{3,2,0,1:T(8,128)(2,1)}, u32[]{:S(2)}, u32[]{:S(2)}) collective-permute-start(bf16[2,2,24,3072]{3,2,0,1:T(8,128)(2,1)} %pad_maximum_fusion.7), channel_id=1, source_target_pairs={{0,1},{1,0},{2,3},{3,2},{4,5},{5,4},{6,7},{7,6},{8,9},{9,8},{10,11... | collective-permute-start | bytes 1769480 | tf_op jit(solution)/shard_map/ppermute | solution.py:933
  104.4 53.1 %collective-permute-start.10 = (bf16[2,2,2,96,768]{4,3,0,1,2:T(8,128)(2,1)}, bf16[2,2,2,96,768]{4,3,0,1,2:T(8,128)(2,1)}, u32[]{:S(2)}, u32[]{:S(2)}) collective-permute-start(bf16[2,2,2,96,768]{4,3,0,1,2:T(8,128)(2,1)} %pad_maximum_fusion.5), channel_id=1, source_target_pairs={{0,16},{16,0},{1,17},{17,1},{2,18},{18,2},{3,19},{19,3},{4,20},{20... | collective-permute-start | bytes 3538952 | tf_op jit(solution)/shard_map/ppermute | solution.py:933
  114.2 38.6 %all-to-all-start.2 = ((bf16[8,3,5,16,384]{4,3,2,1,0:T(8,128)(2,1)}), bf16[8,3,5,16,384]{4,3,2,1,0:T(8,128)(2,1)S(1)}, u32[]{:S(2)}, u32[]{:S(2)}) async-start(bf16[8,3,5,16,384]{4,3,2,1,0:T(8,128)(2,1)} %get-tuple-element.130), calls=%async_computation.2 | async-start | bytes 2949120 | tf_op jit(solution)/shard_map/all_to_all | solution.py:924
  121.6 39.1 %collective-permute-start.7 = (bf16[2,2,2,24,3072]{4,3,0,1,2:T(8,128)(2,1)}, bf16[2,2,2,24,3072]{4,3,0,1,2:T(8,128)(2,1)}, u32[]{:S(2)}, u32[]{:S(2)}) collective-permute-start(bf16[2,2,2,24,3072]{4,3,0,1,2:T(8,128)(2,1)} %pad_maximum_fusion.4), channel_id=1, source_target_pairs={{0,16},{16,0},{1,17},{17,1},{2,18},{18,2},{3,19},{19,3},{4,20},{20... | collective-permute-start | bytes 3538952 | tf_op jit(solution)/shard_map/ppermute | solution.py:933
  152.9 17.9 %all-to-all-start.3 = ((bf16[8,1,5,16,384]{4,3,2,1,0:T(8,128)(2,1)}), bf16[8,1,5,16,384]{4,3,2,1,0:T(8,128)(2,1)}, u32[]{:S(2)}, u32[]{:S(2)}) async-start(bf16[8,1,5,16,384]{4,3,2,1,0:T(8,128)(2,1)} %get-tuple-element.133), calls=%async_computation.3 | async-start | bytes 983040 | tf_op jit(solution)/shard_map/all_to_all | solution.py:924
  160.7 13.4 %collective-permute-start.11 = (bf16[2,2,2,2,96,768]{5,4,1,2,3,0:T(8,128)(2,1)}, bf16[2,2,2,2,96,768]{5,4,1,2,3,0:T(8,128)(2,1)}, u32[]{:S(2)}, u32[]{:S(2)}) collective-permute-start(bf16[2,2,2,2,96,768]{5,4,1,2,3,0:T(8,128)(2,1)} %pad_maximum_fusion.3), channel_id=1, source_target_pairs={{0,8},{8,0},{1,9},{9,1},{2,10},{10,2},{3,11},{11,3},{4,12},{12,4},... | collective-permute-start | bytes 7077896 | tf_op jit(solution)/shard_map/ppermute | solution.py:933
  179.2 32.9 %all-to-all-start.4 = ((bf16[8,2,5,16,384]{4,3,2,1,0:T(8,128)(2,1)}), bf16[8,2,5,16,384]{4,3,2,1,0:T(8,128)(2,1)S(1)}, u32[]{:S(2)}, u32[]{:S(2)}) async-start(bf16[8,2,5,16,384]{4,3,2,1,0:T(8,128)(2,1)} %get-tuple-element.134), calls=%async_computation.4 | async-start | bytes 1966080 | tf_op jit(solution)/shard_map/all_to_all | solution.py:924
  213.1 30.7 %all-to-all-start.5 = ((bf16[8,5,16,768]{3,2,1,0:T(8,128)(2,1)}), bf16[8,5,16,768]{3,2,1,0:T(8,128)(2,1)S(1)}, u32[]{:S(2)}, u32[]{:S(2)}) async-start(bf16[8,5,16,768]{3,2,1,0:T(8,128)(2,1)} %get-tuple-element.157), calls=%async_computation.5 | async-start | bytes 1966080 | tf_op jit(solution)/shard_map/all_to_all | solution.py:924
  243.9 30.1 %all-to-all-start.6 = ((bf16[8,5,16,768]{3,2,1,0:T(8,128)(2,1)}), bf16[8,5,16,768]{3,2,1,0:T(8,128)(2,1)S(1)}, u32[]{:S(2)}, u32[]{:S(2)}) async-start(bf16[8,5,16,768]{3,2,1,0:T(8,128)(2,1)} %get-tuple-element.159), calls=%async_computation.6 | async-start | bytes 1966080 | tf_op jit(solution)/shard_map/all_to_all | solution.py:924
  274.0 36.6 %all-to-all-start.7 = ((bf16[8,5,16,768]{3,2,1,0:T(8,128)(2,1)}), bf16[8,5,16,768]{3,2,1,0:T(8,128)(2,1)S(1)}, u32[]{:S(2)}, u32[]{:S(2)}) async-start(bf16[8,5,16,768]{3,2,1,0:T(8,128)(2,1)} %get-tuple-element.161), calls=%async_computation.7 | async-start | bytes 1966080 | tf_op jit(solution)/shard_map/all_to_all | solution.py:924
  310.6 25.9 %collective-permute-start.12 = (bf16[384,3072]{1,0:T(8,128)(2,1)}, bf16[384,3072]{1,0:T(8,128)(2,1)}, u32[]{:S(2)}, u32[]{:S(2)}) collective-permute-start(bf16[384,3072]{1,0:T(8,128)(2,1)} %get-tuple-element.178), channel_id=1, source_target_pairs={{0,8},{8,0},{1,9},{9,1},{2,10},{10,2},{3,11},{11,3},{4,12},{12,4},... | collective-permute-start | bytes 7077896 | tf_op jit(solution)/shard_map/ppermute | solution.py:933
  310.7 29.9 %collective-permute-start.13 = (bf16[1536,768]{1,0:T(8,128)(2,1)}, bf16[1536,768]{1,0:T(8,128)(2,1)S(1)}, u32[]{:S(2)}, u32[]{:S(2)}) collective-permute-start(bf16[1536,768]{1,0:T(8,128)(2,1)} %bitcast.133), channel_id=1, source_target_pairs={{0,8},{8,0},{1,9},{9,1},{2,10},{10,2},{3,11},{11,3},{4,12},{12,4},... | collective-permute-start | bytes 7077896 | tf_op jit(solution)/shard_map/ppermute | solution.py:933
  330.4 54.1 %all-to-all-start.8 = ((bf16[8,3,5,16,384]{4,3,2,1,0:T(8,128)(2,1)}), bf16[8,3,5,16,384]{4,3,2,1,0:T(8,128)(2,1)}, u32[]{:S(2)}, u32[]{:S(2)}) async-start(bf16[8,3,5,16,384]{4,3,2,1,0:T(8,128)(2,1)} %get-tuple-element.166), calls=%async_computation.8 | async-start | bytes 2949120 | tf_op jit(solution)/shard_map/all_to_all | solution.py:924
  340.1 27.9 %collective-permute-start.15 = (bf16[192,3072]{1,0:T(8,128)(2,1)}, bf16[192,3072]{1,0:T(8,128)(2,1)S(1)}, u32[]{:S(2)}, u32[]{:S(2)}) collective-permute-start(bf16[192,3072]{1,0:T(8,128)(2,1)} %get-tuple-element.180), channel_id=1, source_target_pairs={{0,16},{16,0},{1,17},{17,1},{2,18},{18,2},{3,19},{19,3},{4,20},{20... | collective-permute-start | bytes 3538952 | tf_op jit(solution)/shard_map/ppermute | solution.py:933
  345.5 35.5 %collective-permute-start.14 = (bf16[768,768]{1,0:T(8,128)(2,1)}, bf16[768,768]{1,0:T(8,128)(2,1)S(1)}, u32[]{:S(2)}, u32[]{:S(2)}) collective-permute-start(bf16[768,768]{1,0:T(8,128)(2,1)} %get-tuple-element.184), channel_id=1, source_target_pairs={{0,1},{1,0},{2,3},{3,2},{4,5},{5,4},{6,7},{7,6},{8,9},{9,8},{10,11... | collective-permute-start | bytes 3538952 | tf_op jit(solution)/shard_map/ppermute | solution.py:933
  384.6 49.9 %all-to-all-start.9 = ((bf16[8,3,5,16,384]{4,3,2,1,0:T(8,128)(2,1)}), bf16[8,3,5,16,384]{4,3,2,1,0:T(8,128)(2,1)S(1)}, u32[]{:S(2)}, u32[]{:S(2)}) async-start(bf16[8,3,5,16,384]{4,3,2,1,0:T(8,128)(2,1)} %get-tuple-element.196), calls=%async_computation.9 | async-start | bytes 2949120 | tf_op jit(solution)/shard_map/all_to_all | solution.py:924
  402.2 22.6 %collective-permute-start.23 = (bf16[96,3072]{1,0:T(8,128)(2,1)}, bf16[96,3072]{1,0:T(8,128)(2,1)S(1)}, u32[]{:S(2)}, u32[]{:S(2)}) collective-permute-start(bf16[96,3072]{1,0:T(8,128)(2,1)} %get-tuple-element.195), channel_id=1, source_target_pairs={{0,1},{1,0},{2,3},{3,2},{4,5},{5,4},{6,7},{7,6},{8,9},{9,8},{10,11... | collective-permute-start | bytes 1769480 | tf_op jit(solution)/shard_map/ppermute | solution.py:933
  404.2 27.2 %collective-permute-start.21 = (bf16[384,768]{1,0:T(8,128)(2,1)}, bf16[384,768]{1,0:T(8,128)(2,1)S(1)}, u32[]{:S(2)}, u32[]{:S(2)}) collective-permute-start(bf16[384,768]{1,0:T(8,128)(2,1)} %get-tuple-element.193), channel_id=1, source_target_pairs={{0,16},{16,0},{1,17},{17,1},{2,18},{18,2},{3,19},{19,3},{4,20},{20... | collective-permute-start | bytes 1769480 | tf_op jit(solution)/shard_map/ppermute | solution.py:933
  413.6 20.8 %collective-permute-start.18 = (f32[2,2,25,384]{3,1,2,0:T(2,128)S(1)}, f32[2,2,25,384]{3,1,2,0:T(2,128)S(1)}, u32[]{:S(2)}, u32[]{:S(2)}) collective-permute-start(f32[2,2,25,384]{3,1,2,0:T(2,128)S(1)} %bitcast.127), channel_id=1, source_target_pairs={{0,1},{1,0},{2,3},{3,2},{4,5},{5,4},{6,7},{7,6},{8,9},{9,8},{10,11... | collective-permute-start | bytes 460808 | tf_op jit(solution)/shard_map/ppermute | solution.py:933
  427.7 11.5 %collective-permute-start.24 = (bf16[48,3072]{1,0:T(8,128)(2,1)}, bf16[48,3072]{1,0:T(8,128)(2,1)S(1)}, u32[]{:S(2)}, u32[]{:S(2)}) collective-permute-start(bf16[48,3072]{1,0:T(8,128)(2,1)} %get-tuple-element.219), channel_id=1, source_target_pairs={{0,2},{1,3},{2,0},{3,1},{4,6},{5,7},{6,4},{7,5},{8,10},{9,11},{10,... | collective-permute-start | bytes 884744 | tf_op jit(solution)/shard_map/ppermute | solution.py:933
  434.7 15.4 %collective-permute-start.19 = (f32[2,25,384]{2,0,1:T(2,128)S(1)}, f32[2,25,384]{2,0,1:T(2,128)S(1)}, u32[]{:S(2)}, u32[]{:S(2)}) collective-permute-start(f32[2,25,384]{2,0,1:T(2,128)S(1)} %bitcast.128), channel_id=1, source_target_pairs={{0,2},{1,3},{2,0},{3,1},{4,6},{5,7},{6,4},{7,5},{8,10},{9,11},{10,... | collective-permute-start | bytes 230408 | tf_op jit(solution)/shard_map/ppermute | solution.py:933
  446.4 18.7 %collective-permute-start.26 = (bf16[96,768]{1,0:T(8,128)(2,1)}, bf16[96,768]{1,0:T(8,128)(2,1)S(1)}, u32[]{:S(2)}, u32[]{:S(2)}) collective-permute-start(bf16[96,768]{1,0:T(8,128)(2,1)} %get-tuple-element.225), channel_id=1, source_target_pairs={{0,4},{1,5},{2,6},{3,7},{4,0},{5,1},{6,2},{7,3},{8,12},{9,13},{10,... | collective-permute-start | bytes 442376 | tf_op jit(solution)/shard_map/ppermute | solution.py:933
  450.0 16.3 %collective-permute-start.25 = (bf16[24,3072]{1,0:T(8,128)(2,1)S(1)}, bf16[24,3072]{1,0:T(8,128)(2,1)S(1)}, u32[]{:S(2)}, u32[]{:S(2)}) collective-permute-start(bf16[24,3072]{1,0:T(8,128)(2,1)S(1)} %copy-done.51), channel_id=1, source_target_pairs={{0,4},{1,5},{2,6},{3,7},{4,0},{5,1},{6,2},{7,3},{8,12},{9,13},{10,... | collective-permute-start | bytes 442376 | tf_op jit(solution)/shard_map/ppermute | solution.py:933
  450.3 13.4 %collective-permute-start.20 = (f32[25,384]{1,0:T(8,128)S(1)}, f32[25,384]{1,0:T(8,128)S(1)}, u32[]{:S(2)}, u32[]{:S(2)}) collective-permute-start(f32[25,384]{1,0:T(8,128)S(1)} %bitcast.129), channel_id=1, source_target_pairs={{0,4},{1,5},{2,6},{3,7},{4,0},{5,1},{6,2},{7,3},{8,12},{9,13},{10,... | collective-permute-start | bytes 115208 | tf_op jit(solution)/shard_map/ppermute | solution.py:933
  (57 other events, 424.1 us)
